TPU v7x, 256 devices: a whole 4x4x8 slice. The times are simulated.
256 devices in a mesh: gx: 4 (over y), gy: 4 (over z_lo, core), gz: 16 (over z_hi, x).
Axes of the slice: x: 4, y: 4, z: 8 (z_hi: 4, z_lo: 2; z = z_hi * 2 + z_lo), core: 2. Of those that a mesh axis runs over, the one named last changes fastest.
Arguments:
- positions: float32 [4, 16, 16, 3, 128], P('gx', 'gy', 'gz'), may hold values from 0 to 1
- velocities: float32 [4, 16, 16, 3, 128], P('gx', 'gy', 'gz'), may hold values from -6 to 6
- charges: float32 [4, 16, 16, 128], P('gx', 'gy', 'gz'), may hold values from -3 to 3
- atom_types: int32 [4, 16, 16, 128], P('gx', 'gy', 'gz'), may hold values from 0 to 15
- atom_count: int32 [4, 16, 16], P('gx', 'gy', 'gz'), may hold values from 32 to 128
- sigma_type: float32 [16], replicated, may hold values from 0.15 to 0.35
- epsilon_type: float32 [16], replicated, may hold values from 0.3 to 3
- masses: float32 [4, 16, 16, 128], P('gx', 'gy', 'gz'), may hold values from 1 to 4
- pair_list: int32 [4, 4, 16, 2, 56], P('gx', 'gy', 'gz'), may hold values from 0 to 19, as said below
- pair_count: int32 [4, 4, 16], P('gx', 'gy', 'gz'), may hold values from 1 to 56, as said below
- pos_cotangent: float32 [4, 16, 16, 3, 128], P('gx', 'gy', 'gz'), may hold values from -6 to 6
- vel_cotangent: float32 [4, 16, 16, 3, 128], P('gx', 'gy', 'gz'), may hold values from -6 to 6
Outputs:
- pos_final: float32 [4, 16, 16, 3, 128], P('gx', 'gy', 'gz')
- vel_final: float32 [4, 16, 16, 3, 128], P('gx', 'gy', 'gz')
- grad_pos: float32 [4, 16, 16, 3, 128], P('gx', 'gy', 'gz')
- grad_vel: float32 [4, 16, 16, 3, 128], P('gx', 'gy', 'gz')
- grad_charge: float32 [4, 16, 16, 128], P('gx', 'gy', 'gz')
Inputs may be any that keep to these rules, and one draw needn't show every extreme that they name: `pair_list`: for k < pair_count[a, b, c] the two extended indices of slot k name blocks inside the global grid of 4 x 16 x 16 blocks, their coordinates differ by at most one in each dimension, and their smaller coordinate in each dimension lies in the device's own blocks; an unordered pair of blocks appears in at most one live slot over all devices. Slots at and past the count hold indices in range and are ignored. `pair_count`: some device has all 56 slots live in every draw.
All inputs are finite; a program needn't handle non-finite values.
Results may differ from a plain program's by a relative error of at most 0.00027.
Values sent between devices are 32-bit elements; how exact they have to be, the bound alone decides.
No kernel may reach another device: no remote copies, remote signals or barrier semaphores. Data moves between devices by JAX's collectives and lax.ppermute only.
A program may use at most 64 MiB of HBM per device.

v0:
```python
import jax
import jax.numpy as jnp
from jax import lax
from jax.sharding import PartitionSpec as P

STEPS = 5


SOFT = 0.04
KAPPA = 2.0
COULOMB = 4.0
TIME_STEP = 0.004


def passed_along(value, axis, steps):
    count = lax.axis_size(axis)
    leading, last = (max(0, -steps), min(count, count - steps))
    return lax.ppermute(value, axis, [(source, source + steps) for source in range(leading, last)])


def tile_energy(
    left_pos,
    right_pos,
    left_charge,
    right_charge,
    left_sigma,
    right_sigma,
    left_depth,
    right_depth,
    offset,
    same_block,
):
    separation = left_pos[:, :, None] - right_pos[:, None, :] + offset[:, None, None]
    distance = jnp.sum(separation * separation, axis=0)
    mean_sigma = 0.5 * (left_sigma[:, None] + right_sigma[None, :])
    squared_sigma = mean_sigma * mean_sigma
    fraction = squared_sigma / (distance + squared_sigma)
    third_power = fraction * fraction * fraction
    dispersion = (
        4.0 * left_depth[:, None] * right_depth[None, :] * (third_power * third_power - third_power)
    )
    radius = jnp.sqrt(distance + SOFT)
    screened = (
        COULOMB * left_charge[:, None] * right_charge[None, :] * jnp.exp(-KAPPA * radius) / radius
    )
    fading = jnp.maximum(1.0 - distance, 0.0)
    switch = fading * fading * fading
    per_block = left_pos.shape[1]
    diagonal = (
        lax.broadcasted_iota(jnp.int32, (per_block, per_block), 0)
        == lax.broadcasted_iota(jnp.int32, (per_block, per_block), 1)
    ).astype(jnp.float32)
    weight = 1.0 - same_block * (0.5 + 0.5 * diagonal)
    return jnp.sum(weight * switch * (dispersion + screened))


def tile_forces(
    left_pos,
    right_pos,
    left_charge,
    right_charge,
    left_sigma,
    right_sigma,
    left_depth,
    right_depth,
    offset,
    same_block,
):
    gradients = jax.grad(tile_energy, argnums=(0, 1))(
        left_pos,
        right_pos,
        left_charge,
        right_charge,
        left_sigma,
        right_sigma,
        left_depth,
        right_depth,
        offset,
        same_block,
    )
    return (-gradients[0], -gradients[1])


def pair_terms(flat_pos, flat_par, flat_cot, first_ids, second_ids, offset, same_block, live_slot):
    left_pos = jnp.take(flat_pos, first_ids, axis=0)
    right_pos = jnp.take(flat_pos, second_ids, axis=0)
    left_par = jnp.take(flat_par, first_ids, axis=0)
    right_par = jnp.take(flat_par, second_ids, axis=0)
    slot_mask = live_slot[:, None, None]

    def batch_forces(pos_one, pos_two, charge_one, charge_two):
        return jax.vmap(tile_forces)(
            pos_one,
            pos_two,
            charge_one,
            charge_two,
            left_par[:, 1],
            right_par[:, 1],
            left_par[:, 2],
            right_par[:, 2],
            offset,
            same_block,
        )

    if flat_cot is None:
        left_force, right_force = batch_forces(left_pos, right_pos, left_par[:, 0], right_par[:, 0])
        return (left_force * slot_mask, right_force * slot_mask)
    results, pullback = jax.vjp(batch_forces, left_pos, right_pos, left_par[:, 0], right_par[:, 0])
    left_cot = jnp.take(flat_cot, first_ids, axis=0) * slot_mask
    right_cot = jnp.take(flat_cot, second_ids, axis=0) * slot_mask
    pulled = pullback((left_cot, right_cot))
    left_rows = [pulled[0], pulled[2][:, None, :]]
    right_rows = [pulled[1], pulled[3][:, None, :]]
    return (jnp.concatenate(left_rows, axis=1), jnp.concatenate(right_rows, axis=1))


def atom_params(charges, atom_types, atom_count, sigma_type, epsilon_type):
    type_total = sigma_type.shape[0]
    alive_mask = (
        lax.broadcasted_iota(jnp.int32, charges.shape, charges.ndim - 1) < atom_count[..., None]
    ).astype(jnp.float32)
    matches = (
        atom_types[..., None, :] == lax.broadcasted_iota(jnp.int32, (type_total, 1), 0)
    ).astype(jnp.float32)
    sigma_atom = jnp.sum(matches * sigma_type[:, None], axis=-2)
    depth_atom = jnp.sum(matches * epsilon_type[:, None], axis=-2)
    params = jnp.stack(
        [charges * alive_mask, sigma_atom, jnp.sqrt(depth_atom) * alive_mask], axis=-2
    )
    return (alive_mask, params)


def rim_import(field):
    upper = passed_along(field, "gx", -1)
    field = jnp.concatenate([field, upper], axis=0)
    upper = passed_along(field[:, :1], "gy", -1)
    field = jnp.concatenate([field, upper], axis=1)
    upper = passed_along(field, "gz", -1)
    return jnp.concatenate([field, upper], axis=2)


def rim_return(field):
    lower = passed_along(field[:, :, -1:], "gz", 1)
    field = jnp.concatenate([field[:, :, :1] + lower, field[:, :, 1:-1]], axis=2)
    lower = passed_along(field[:, -1:], "gy", 1)
    field = jnp.concatenate([field[:, :1] + lower, field[:, 1:-1]], axis=1)
    lower = passed_along(field[-1:], "gx", 1)
    return jnp.concatenate([field[:1] + lower, field[1:-1]], axis=0)


def sweep(ext_pos, ext_par, pair_list, pair_count, ext_cot):
    extent_x, extent_y, extent_z, unused, per_block = ext_pos.shape
    ext_total = extent_x * extent_y * extent_z
    flat_pos = ext_pos.reshape(ext_total, 3, per_block)
    flat_par = ext_par.reshape(ext_total, 3, per_block)
    flat_cot = None if ext_cot is None else ext_cot.reshape(ext_total, 3, per_block)
    first_all = pair_list[0, 0, 0, 0]
    second_all = pair_list[0, 0, 0, 1]
    slot_total = first_all.shape[0]
    own_cells = slot_total // 14
    group = 14 * max(1, own_cells // 8)

    def local_coords(index):
        return (index // (extent_y * extent_z), index // extent_z % extent_y, index % extent_z)

    left_local = local_coords(first_all)
    right_local = local_coords(second_all)
    offset_all = jnp.stack(
        [(left_local[column] - right_local[column]).astype(jnp.float32) for column in range(3)],
        axis=-1,
    )
    same_all = (first_all == second_all).astype(jnp.float32)
    live_pairs = pair_count[0, 0, 0]
    live_all = (lax.broadcasted_iota(jnp.int32, (slot_total,), 0) < live_pairs).astype(jnp.float32)
    rows_total = 3 if ext_cot is None else 4
    block_rows = lax.broadcasted_iota(jnp.int32, (ext_total, group), 0)

    def one_batch(batch_index, totals):
        first_row = batch_index * group
        first_ids = lax.dynamic_slice_in_dim(first_all, first_row, group)
        second_ids = lax.dynamic_slice_in_dim(second_all, first_row, group)
        offset = lax.dynamic_slice_in_dim(offset_all, first_row, group)
        same_block = lax.dynamic_slice_in_dim(same_all, first_row, group)
        live_slot = lax.dynamic_slice_in_dim(live_all, first_row, group)
        left_rows, right_rows = pair_terms(
            flat_pos, flat_par, flat_cot, first_ids, second_ids, offset, same_block, live_slot
        )
        left_select = (first_ids[None, :] == block_rows).astype(jnp.float32)
        right_select = (second_ids[None, :] == block_rows).astype(jnp.float32)
        totals = totals + jnp.dot(
            left_select,
            left_rows.reshape(group, rows_total * per_block),
            precision=lax.Precision.HIGHEST,
            preferred_element_type=jnp.float32,
        )
        return totals + jnp.dot(
            right_select,
            right_rows.reshape(group, rows_total * per_block),
            precision=lax.Precision.HIGHEST,
            preferred_element_type=jnp.float32,
        )

    rounds = slot_total // group
    initial = jnp.zeros((ext_total, rows_total * per_block), jnp.float32)
    totals = lax.fori_loop(0, rounds, one_batch, initial)
    return totals.reshape(extent_x, extent_y, extent_z, rows_total, per_block)


def on_device(
    positions,
    velocities,
    charges,
    atom_types,
    atom_count,
    sigma_type,
    epsilon_type,
    masses,
    pair_list,
    pair_count,
    pos_cotangent,
    vel_cotangent,
):
    alive_mask, params = atom_params(charges, atom_types, atom_count, sigma_type, epsilon_type)
    inverse = (1.0 / masses)[..., None, :]
    half_step = 0.5 * TIME_STEP
    extended = rim_import(jnp.concatenate([positions, params], axis=3))
    ext_pos = extended[:, :, :, :3]
    ext_par = extended[:, :, :, 3:]
    history = [ext_pos]
    forces = rim_return(sweep(ext_pos, ext_par, pair_list, pair_count, None))
    position = positions
    velocity = velocities
    grad_position = pos_cotangent
    grad_velocity = vel_cotangent
    for step_index in range(STEPS):
        plain_position = position
        plain_forces = forces
        midway = velocity + half_step * inverse * plain_forces
        plain_position = plain_position + TIME_STEP * midway
        ext_next = rim_import(plain_position)
        plain_forces = rim_return(sweep(ext_next, ext_par, pair_list, pair_count, None))
        position, velocity, forces, ext_next = (
            plain_position,
            midway + half_step * inverse * plain_forces,
            plain_forces,
            ext_next,
        )
        history.append(ext_next)
    last_cot = rim_import(half_step * inverse * grad_velocity)
    pulled = rim_return(sweep(history[STEPS], ext_par, pair_list, pair_count, last_cot))
    grad_position = grad_position + pulled[:, :, :, :3]
    charge_sum = pulled[:, :, :, 3]
    for step_index in range(STEPS - 1, -1, -1):
        grad_velocity = grad_velocity + TIME_STEP * grad_position
        factor = TIME_STEP if step_index > 0 else half_step
        ext_cot = rim_import(factor * inverse * grad_velocity)
        pulled = rim_return(sweep(history[step_index], ext_par, pair_list, pair_count, ext_cot))
        grad_position = grad_position + pulled[:, :, :, :3]
        charge_sum = charge_sum + pulled[:, :, :, 3]
    return (position, velocity, grad_position, grad_velocity, charge_sum * alive_mask)


def solution(mesh):
    in_specs = (
        P("gx", "gy", "gz", None, None),
        P("gx", "gy", "gz", None, None),
        P("gx", "gy", "gz", None),
        P("gx", "gy", "gz", None),
        P("gx", "gy", "gz"),
        P(),
        P(),
        P("gx", "gy", "gz", None),
        P("gx", "gy", "gz", None, None),
        P("gx", "gy", "gz"),
        P("gx", "gy", "gz", None, None),
        P("gx", "gy", "gz", None, None),
    )
    out_specs = (
        P("gx", "gy", "gz", None, None),
        P("gx", "gy", "gz", None, None),
        P("gx", "gy", "gz", None, None),
        P("gx", "gy", "gz", None, None),
        P("gx", "gy", "gz", None),
    )
    return jax.shard_map(
        on_device, mesh=mesh, in_specs=in_specs, out_specs=out_specs, check_vma=False
    )
```

profile of v0, /device:TPU:96, one launch (start us, length us, event | category | flops | bytes accessed | tf_op | source)
XLA Modules:
  0.0 982.2 jit_solution(3404316550937150910)
XLA Ops:
  20.5 35.9 %while.180 = (s32[]{:T(128)}, f32[20,384]{1,0:T(8,128)S(1)}, s32[56]{0:T(128)S(1)}, f32[20,3,128]{2,1,0:T(4,128)S(1)}, s32[56]{0:T(128)S(1)}, /*index=5*/f32[56,...) while((s32[]{:T(128)}, f32[20,384]{1,0:T(8,128)S(1)}, ...), condition=%wide.region_6.8_spmd.clone.clone, body=%wide.region_2.7_spmd.clone.clone.sunk | while | flops 24247344 | bytes 4899005 | solution.py:205
  89.6 35.8 %while.181 = (s32[]{:T(128)}, f32[20,384]{1,0:T(8,128)S(1)}, s32[56]{0:T(128)S(1)}, f32[20,3,128]{2,1,0:T(4,128)S(1)}, s32[56]{0:T(128)S(1)}, /*index=5*/f32[56,...) while((s32[]{:T(128)}, f32[20,384]{1,0:T(8,128)S(1)}, ...), condition=%wide.region_11.13_spmd.clone.clone, body=%wide.region_7.12_spmd.clone.clone.sunk | while | flops 24247344 | bytes 4899005 | solution.py:205
  159.2 35.9 %while.182 = (s32[]{:T(128)}, f32[20,384]{1,0:T(8,128)S(1)}, s32[56]{0:T(128)S(1)}, f32[20,3,128]{2,1,0:T(4,128)S(1)}, s32[56]{0:T(128)S(1)}, /*index=5*/f32[56,...) while((s32[]{:T(128)}, f32[20,384]{1,0:T(8,128)S(1)}, ...), condition=%wide.region_16.18_spmd.clone.clone, body=%wide.region_12.17_spmd.clone.clone.sunk | while | flops 24247344 | bytes 4899005 | solution.py:205
  228.7 35.9 %while.183 = (s32[]{:T(128)}, f32[20,384]{1,0:T(8,128)S(1)}, s32[56]{0:T(128)S(1)}, f32[20,3,128]{2,1,0:T(4,128)S(1)}, s32[56]{0:T(128)S(1)}, /*index=5*/f32[56,...) while((s32[]{:T(128)}, f32[20,384]{1,0:T(8,128)S(1)}, ...), condition=%wide.region_21.23_spmd.clone.clone, body=%wide.region_17.22_spmd.clone.clone.sunk | while | flops 24247344 | bytes 4899005 | solution.py:205
  298.3 35.9 %while.184 = (s32[]{:T(128)}, f32[20,384]{1,0:T(8,128)S(1)}, s32[56]{0:T(128)S(1)}, f32[20,3,128]{2,1,0:T(4,128)S(1)}, s32[56]{0:T(128)S(1)}, /*index=5*/f32[56,...) while((s32[]{:T(128)}, f32[20,384]{1,0:T(8,128)S(1)}, ...), condition=%wide.region_26.28_spmd.clone.clone, body=%wide.region_22.27_spmd.clone.clone.sunk | while | flops 24247344 | bytes 4899005 | solution.py:205
  334.2 6.6 collective-permute-start.27
  370.7 62.7 %while.186 = (s32[]{:T(128)}, f32[20,512]{1,0:T(8,128)S(1)}, s32[56]{0:T(128)S(1)}, f32[20,3,128]{2,1,0:T(4,128)S(1)}, s32[56]{0:T(128)S(1)}, /*index=5*/f32[56,...) while((s32[]{:T(128)}, f32[20,512]{1,0:T(8,128)S(1)}, ...), condition=%wide.region_39.41_spmd.clone.clone, body=%wide.region_32.40_spmd.clone.clone.sunk | while | flops 55421488 | bytes 10967293 | solution.py:205
  376.7 6.0 fusion.675
  392.4 6.0 fusion.675
  408.1 6.0 fusion.675
  423.8 6.0 fusion.675
  433.5 6.0 collective-permute-start.39
  467.2 62.7 %while.187 = (s32[]{:T(128)}, f32[20,512]{1,0:T(8,128)S(1)}, s32[56]{0:T(128)S(1)}, f32[20,3,128]{2,1,0:T(4,128)S(1)}, s32[56]{0:T(128)S(1)}, /*index=5*/f32[56,...) while((s32[]{:T(128)}, f32[20,512]{1,0:T(8,128)S(1)}, ...), condition=%wide.region_47.49_spmd.clone.clone, body=%wide.region_40.48_spmd.clone.clone.sunk | while | flops 55421488 | bytes 10967293 | solution.py:205
  473.2 6.0 fusion.680
  530.0 7.2 collective-permute-start.45
  563.9 62.7 %while.188 = (s32[]{:T(128)}, f32[20,512]{1,0:T(8,128)S(1)}, s32[56]{0:T(128)S(1)}, f32[20,3,128]{2,1,0:T(4,128)S(1)}, s32[56]{0:T(128)S(1)}, /*index=5*/f32[56,...) while((s32[]{:T(128)}, f32[20,512]{1,0:T(8,128)S(1)}, ...), condition=%wide.region_55.57_spmd.clone.clone, body=%wide.region_48.56_spmd.clone.clone.sunk | while | flops 55421488 | bytes 10967293 | solution.py:205
  626.7 8.2 collective-permute-start.51
  661.6 62.7 %while.189 = (s32[]{:T(128)}, f32[20,512]{1,0:T(8,128)S(1)}, s32[56]{0:T(128)S(1)}, f32[20,3,128]{2,1,0:T(4,128)S(1)}, s32[56]{0:T(128)S(1)}, /*index=5*/f32[56,...) while((s32[]{:T(128)}, f32[20,512]{1,0:T(8,128)S(1)}, ...), condition=%wide.region_63.65_spmd.clone.clone, body=%wide.region_56.64_spmd.clone.clone.sunk | while | flops 55421488 | bytes 10967293 | solution.py:205
  724.4 8.2 collective-permute-start.57
  755.2 35.8 %while.185 = (s32[]{:T(128)}, f32[20,384]{1,0:T(8,128)S(1)}, s32[56]{0:T(128)S(1)}, f32[20,3,128]{2,1,0:T(4,128)S(1)}, s32[56]{0:T(128)S(1)}, /*index=5*/f32[56,...) while((s32[]{:T(128)}, f32[20,384]{1,0:T(8,128)S(1)}, ...), condition=%wide.region_31.33_spmd.clone.clone, body=%wide.region_27.32_spmd.clone.clone.sunk | while | flops 24247344 | bytes 4899005 | solution.py:205
  795.6 62.7 %while.190 = (s32[]{:T(128)}, f32[20,512]{1,0:T(8,128)S(1)}, s32[56]{0:T(128)S(1)}, f32[20,3,128]{2,1,0:T(4,128)S(1)}, s32[56]{0:T(128)S(1)}, /*index=5*/f32[56,...) while((s32[]{:T(128)}, f32[20,512]{1,0:T(8,128)S(1)}, ...), condition=%wide.region_71.73_spmd.clone.clone, body=%wide.region_64.72_spmd.clone.clone.sunk | while | flops 55421488 | bytes 10967293 | solution.py:205
  858.4 8.1 collective-permute-start.63
  897.3 62.7 %while.191 = (s32[]{:T(128)}, f32[20,512]{1,0:T(8,128)S(1)}, s32[56]{0:T(128)S(1)}, f32[20,3,128]{2,1,0:T(4,128)S(1)}, s32[56]{0:T(128)S(1)}, /*index=5*/f32[56,...) while((s32[]{:T(128)}, f32[20,512]{1,0:T(8,128)S(1)}, ...), condition=%wide.region_79.81_spmd.clone.clone, body=%wide.region_72.80_spmd.clone.clone.sunk | while | flops 55421488 | bytes 10967293 | solution.py:205
  960.1 8.1 collective-permute-start.69
  (2065 shorter events, 884.8 us)
Async XLA Ops:
  56.4 8.7 collective-permute-start.3
  74.9 5.8 collective-permute-start.6
  125.5 8.7 collective-permute-start.9
  144.4 5.8 collective-permute-start.12
  195.1 8.7 collective-permute-start.15
  214.0 5.8 collective-permute-start.18
  264.7 8.7 collective-permute-start.21
  283.6 5.8 collective-permute-start.24
  334.2 8.7 collective-permute-start.27
  353.2 6.2 collective-permute-start.30
  361.3 6.0 collective-permute-start.38
  433.5 8.7 collective-permute-start.39
  452.5 5.8 collective-permute-start.42
  530.0 8.7 collective-permute-start.45
  558.0 5.9 collective-permute-start.50
  626.7 9.7 collective-permute-start.51
  655.7 6.0 collective-permute-start.56
  724.4 9.7 collective-permute-start.57
  753.3 42.3 %collective-permute-start.62 = (f32[2,5,1,3,128]{4,3,2,1,0:T(4,128)S(1)}, f32[2,5,1,3,128]{4,3,2,1,0:T(4,128)S(1)}, u32[]{:S(2)}, u32[]{:S(2)}) collective-permute-start(f32[2,5,1,3,128]{4,3,2,1,0:T(4,128)S(1)} %pad_maximum_fusion.34), channel_id=1, source_target_pairs={{1,0},{2,1},{3,2},{4,3},{5,4},{6,5},{7,6},{8,7},{9,8},{10,9},{11,1... | collective-permute-start | bytes 46088 | tf_op jit(solution)/shard_map/ppermute | solution.py:18
  791.1 75.4 %collective-permute-start.33 = (f32[2,5,1,3,128]{4,3,2,1,0:T(4,128)S(1)}, f32[2,5,1,3,128]{4,3,2,1,0:T(4,128)S(1)}, u32[]{:S(2)}, u32[]{:S(2)}) collective-permute-start(f32[2,5,1,3,128]{4,3,2,1,0:T(4,128)S(1)} %slice.1348), channel_id=1, source_target_pairs={{0,1},{1,2},{2,3},{3,4},{4,5},{5,6},{6,7},{7,8},{8,9},{9,10},{10,1... | collective-permute-start | bytes 46088 | tf_op jit(solution)/shard_map/ppermute | solution.py:18
  858.4 10.1 %collective-permute-start.63 = (f32[2,5,1,4,128]{4,3,2,1,0:T(4,128)S(1)}, f32[2,5,1,4,128]{4,3,2,1,0:T(4,128)S(1)}, u32[]{:S(2)}, u32[]{:S(2)}) collective-permute-start(f32[2,5,1,4,128]{4,3,2,1,0:T(4,128)S(1)} %slice.1387), channel_id=1, source_target_pairs={{0,1},{1,2},{2,3},{3,4},{4,5},{5,6},{6,7},{7,8},{8,9},{9,10},{10,1... | collective-permute-start | bytes 61448 | tf_op jit(solution)/shard_map/ppermute | solution.py:18
  873.5 7.4 collective-permute-start.65
  891.3 6.0 collective-permute-start.68
  960.1 9.6 collective-permute-start.69
  (54 other events, 608.4 us)
where the time goes:
time: 1000 us; the launch traced here: 982 us
  other arithmetic  419 us (42%)
  starting transfers between devices  216 us (22%)
  waiting for transfers between devices  160 us (16%)
  local copies, waits for them, and re-layouts  155 us (16%)
  matrix products  17.1 us (2%)
  loops' own time  11.7 us (1%)
    ppermute x72, starting transfers between devices, passed_along(): lax.ppermute(value, axis, [(source, source + steps) for source in range(l...  216 us
    add_any x48, other arithmetic, tile_energy(): fraction = squared_sigma / (distance + squared_sigma)  206 us
    ppermute x72, waiting for transfers between devices, passed_along(): lax.ppermute(value, axis, [(source, source + steps) for source in range(l...  160 us
    reduce_sum x48, other arithmetic, tile_energy(): left_pos[:, :, None] - right_pos[:, None, :] + offset[:, None, None]  107 us
    reduce_sum x48, other arithmetic, tile_energy(): distance = jnp.sum(separation * separation, axis=0)  69.6 us
    gather x48, local copies, waits for them, and re-layouts, pair_terms(): right_par = jnp.take(flat_par, second_ids, axis=0)  28.1 us
    gather x48, local copies, waits for them, and re-layouts, pair_terms(): left_par = jnp.take(flat_par, first_ids, axis=0)  28.1 us
    gather x48, local copies, waits for them, and re-layouts, pair_terms(): right_pos = jnp.take(flat_pos, second_ids, axis=0)  28.1 us
  transfers between devices with their start and end apart: 72, of which 62 were waited for; matrix products, arithmetic and copies ran while one was open for 10% of the time, Pallas kernels for 0%

commit v1 on v0

v1 whole, which is shorter than its diff:
```python
import functools

import jax
import jax.numpy as jnp
from jax import lax
from jax.experimental import pallas as pl
from jax.experimental.pallas import tpu as pltpu
from jax.sharding import PartitionSpec as P

STEPS = 5
SOFT = 0.04
KAPPA = 2.0
COULOMB = 4.0
TIME_STEP = 0.004
HALF = 0.5 * TIME_STEP
AXES = ("gx", "gy", "gz")
GRID = 16
BLOCKS = 16
ROWS = 18
TILES = 4
GROUP = 8 * TILES


def column_device(y, z):
    phys_y = y // 4
    phys_x = y % 4 if phys_y % 2 == 0 else 3 - y % 4
    phys_z = z // 2
    core = z % 2 if phys_z % 2 == 0 else 1 - z % 2
    return (phys_y * 4 + (phys_z % 2) * 2 + core) * 16 + (phys_z // 2) * 4 + phys_x


def column_of_device():
    gx, gy, gz = (lax.axis_index(name) for name in AXES)
    low, core = gy // 2, gy % 2
    high, phys_x = gz // 4, gz % 4
    phys_z = high * 2 + low
    y = gx * 4 + jnp.where(gx % 2 == 0, phys_x, 3 - phys_x)
    z = phys_z * 2 + jnp.where(phys_z % 2 == 0, core, 1 - core)
    return y, z


def spread_pairs(turn):
    return [
        ((a * 4 + b) * 16 + c, column_device(4 * b + (a + turn) % 4, c))
        for a in range(4)
        for b in range(4)
        for c in range(16)
    ]


def swap_pairs(axis, parity):
    pairs = []
    for y in range(GRID):
        for z in range(GRID):
            own = (y, z)[axis]
            other = own + 1 if own % 2 == parity else own - 1
            if 0 <= other < GRID:
                target = (other, z) if axis == 0 else (y, other)
                pairs.append((column_device(y, z), column_device(*target)))
    return pairs


def down_pairs(axis):
    pairs = []
    for y in range(GRID):
        for z in range(GRID):
            target = (y - 1, z) if axis == 0 else (y, z - 1)
            if min(target) >= 0:
                pairs.append((column_device(y, z), column_device(*target)))
    return pairs


def send(value, pairs):
    return lax.ppermute(value, AXES, pairs)


def list_kernel(list_ref, count_ref, place_ref, out_ref, total_ref):
    y_in_four, y_role, z_role = place_ref[0], place_ref[1], place_ref[2]
    total = jnp.int32(0)
    for a in range(4):

        def one(k, total, a=a):
            def block(index):
                i = (index * 205) >> 11
                j = (index - 10 * i) >> 1
                return a + i, j, index & 1

            def number(x, j, l):
                return (((((j - y_in_four) & 1) ^ y_role) * 2 + (l ^ z_role)) * 4) + jnp.minimum(x, 3)

            first = block(list_ref[a, k])
            second = block(list_ref[a, 56 + k])
            mine = jnp.minimum(first[1], second[1]) == y_in_four
            one_number, two_number = number(*first), number(*second)
            one_count, two_count = count_ref[one_number], count_ref[two_number]
            swap = one_count > two_count
            sign = jnp.where(swap, -1, 1)
            left = jnp.where(swap, two_number, one_number)
            right = jnp.where(swap, one_number, two_number)
            steps = (jnp.minimum(one_count, two_count) + (GROUP - 1)) // GROUP
            word = left + right * 16 + steps * 256
            for place in range(3):
                word = word + ((sign * (first[place] - second[place]) + 1) << (13 + 2 * place))
            out_ref[total] = word
            return total + jnp.where(mine, 1, 0)

        total = lax.fori_loop(0, jnp.minimum(list_ref[a, 112], 56), one, total)
    total_ref[0] = total


def inverse_of(value):
    guess = pl.reciprocal(value, approx=True)
    return guess * (2.0 - value * guess)


def sweep_tiles(mode, list_ref, total_ref, rows_ref, columns_ref, row_sum_ref, column_sum_ref):
    forces, pulled = "F" in mode, "J" in mode
    made = 3 * forces + 4 * pulled
    lane = lax.broadcasted_iota(jnp.int32, (8, 128), 1)

    def one_pair(k, carry):
        word = list_ref[k]
        left, right, steps = word & 15, (word >> 4) & 15, (word >> 8) & 31
        offset = [(((word >> (13 + 2 * c)) & 3) - 1).astype(jnp.float32) for c in range(3)]
        weight = jnp.where(left == right, 0.5, 1.0).astype(jnp.float32)

        def row(c, scale=None, shift=None):
            value = rows_ref[right, pl.ds(c, 1), :]
            if scale is not None:
                value = value * scale
            if shift is not None:
                value = value - shift
            return jnp.broadcast_to(value, (8, 128))

        right_pos = [row(c, shift=offset[c]) for c in range(3)]
        right_charge = row(3, scale=weight)
        right_half = row(4)
        right_depth = row(5, scale=weight)
        right_cot = [row(6 + c) for c in range(3)] if pulled else None

        def one_step(step, sums):
            sums = list(sums)
            for tile in range(TILES):
                first_row = pl.multiple_of(step * GROUP + 8 * tile, 8)
                packed = columns_ref[left, pl.ds(first_row, 8), :]

                def column(c):
                    return jnp.broadcast_to(packed[:, c : c + 1], (8, 128))

                d = [column(c) - right_pos[c] for c in range(3)]
                charge = column(3)
                half = column(4) + right_half
                depth = column(5) * right_depth
                s = d[0] * d[0] + d[1] * d[1] + d[2] * d[2]
                sigma2 = half * half
                r = inverse_of(s + sigma2)
                t = sigma2 * r
                p = t * t * t
                soft = s + SOFT
                ir = lax.rsqrt(soft)
                g = jnp.exp((soft * ir) * -KAPPA) * ir
                fade = jnp.maximum(1.0 - s, 0.0)
                fade2 = fade * fade
                fr = fade * r
                kappa_term = ir + 0.5 * (ir * ir)
                h = g * (3.0 + fade * kappa_term)
                dp = depth * p
                twop = 2.0 * p - 1.0
                charges = charge * right_charge
                A = (fade2 * 8.0) * (3.0 * dp * ((p - 1.0) + fr * twop) + charges * h)
                values = []
                if forces:
                    values += [A * d[c] for c in range(3)]
                if pulled:
                    w = [column(6 + c) - right_cot[c] for c in range(3)]
                    dw = d[0] * w[0] + d[1] * w[1] + d[2] * w[2]
                    ir2 = ir * ir
                    lj = (6.0 * dp) * ((p - 1.0) + fr * (3.0 * twop + fr * (7.0 * p - 2.0)))
                    m2 = ir2 * (1.0 + 1.5 * ir + 0.75 * ir2)
                    cb = (charges * g) * (6.0 + fade * (6.0 * kappa_term + fade * m2))
                    B = (-16.0 * fade) * (lj + cb) * dw
                    values += [A * w[c] + B * d[c] for c in range(3)]
                    common = (8.0 * fade2) * h * dw
                    values += [common * right_charge]
                    last = common * charge * weight
                packed_sum = None
                for place, value in enumerate(values):
                    total = jnp.sum(value, axis=1, keepdims=True)
                    total = jnp.broadcast_to(total, (8, 128))
                    packed_sum = total if place == 0 else jnp.where(lane == place, total, packed_sum)
                here = (left, pl.ds(first_row, 8), slice(None))
                row_sum_ref[here] = row_sum_ref[here] + packed_sum
                if pulled:
                    values[-1] = -last
                sums = [a + b for a, b in zip(sums, values)]
            return tuple(sums)

        zero = jnp.zeros((8, 128), jnp.float32)
        sums = lax.fori_loop(0, steps, one_step, (zero,) * made)
        for place in range(made):
            column_sum_ref[place, right] = column_sum_ref[place, right] + sums[place]
        return carry

    lax.fori_loop(0, total_ref[0], one_pair, jnp.int32(0))


def sweep_kernel(mode, first, kick, list_ref, total_ref, *refs):
    forces, pulled = "F" in mode, "J" in mode
    made = 3 * forces + 4 * pulled
    names = ["ext"]
    if mode != "J":
        names += ["x", "v"] if not first else []
        names += [] if first else ["C", "rC", "D", "rD"]
    else:
        names += ["x", "ax", "av", "C", "rC", "D", "rD", "charge"] + (["v"] if first else [])
    outs = ["A", "B"]
    if mode == "F" and not first:
        outs += ["x_out", "v_out"]
    if mode == "FJ":
        outs += ["x_out", "v_out", "charge_out"]
    if mode == "J":
        outs += ["ax_out", "av_out", "charge_out"] + (["v_out"] if first else [])
    scratch = ["rows", "columns", "row_sum", "column_sum"]
    r = dict(zip(names + outs + scratch, refs))
    ext = r["ext"]
    inverse = ext[9]

    def received(c):
        return jnp.concatenate([r["C"][c] + r["rC"][c], r["D"][c] + r["rD"][c]], axis=0)

    position, cotangent = [], []
    for c in range(3):
        if mode != "J":
            if first:
                position.append(ext[c])
            else:
                velocity = r["v"][c] + kick * inverse * received(c)
                position.append(r["x"][c] + TIME_STEP * velocity)
                r["x_out"][c] = position[c]
                r["v_out"][c] = velocity
            if pulled:
                cotangent.append(HALF * inverse * ext[13 + c])
        else:
            if first:
                r["v_out"][c] = r["v"][c] + HALF * inverse * received(c)
            ax = r["ax"][c] + received(c + 3 if first else c)
            av = r["av"][c] + TIME_STEP * ax
            r["ax_out"][c] = ax
            r["av_out"][c] = av
            position.append(r["x"][c])
            cotangent.append(kick * inverse * av)
    _spread_and_sweep(mode, ext, position, cotangent, list_ref, total_ref, r, made, pulled)


def _spread_and_sweep(mode, ext, position, cotangent, list_ref, total_ref, r, made, pulled):
    rows = r["rows"]
    quantities = position + [ext[6], 0.5 * ext[7], ext[8]] + cotangent
    for place, value in enumerate(quantities):
        for e in range(BLOCKS):
            rows[e, place : place + 1, :] = value[e : e + 1, :]
    for e in range(BLOCKS):
        r["columns"][e, :, 0:16] = rows[e].T
        r["row_sum"][e] = jnp.zeros((128, 128), jnp.float32)
    r["column_sum"][...] = jnp.zeros(r["column_sum"].shape, jnp.float32)
    sweep_tiles(mode, list_ref, total_ref, rows, r["columns"], r["row_sum"], r["column_sum"])
    for e in range(BLOCKS):
        by_row = r["row_sum"][e].T
        target = r["A"] if (e // 4) % 2 == 0 else r["B"]
        place = (e // 8) * 4 + e % 4
        for c in range(made):
            total = by_row[c : c + 1] - jnp.sum(r["column_sum"][c, e], axis=0, keepdims=True)
            if pulled and c == made - 1:
                if mode == "J":
                    total = total + r["charge"][e : e + 1, :]
                r["charge_out"][e : e + 1, :] = total
            else:
                target[c, place : place + 1, :] = total


def sweep(mode, first, kick, plist, total, arrays):
    forces, pulled = "F" in mode, "J" in mode
    sent = 3 * forces + 3 * pulled
    made = 3 * forces + 4 * pulled
    f32 = jnp.float32
    exchange = jax.ShapeDtypeStruct((sent, 8, 128), f32)
    vector = jax.ShapeDtypeStruct((3, BLOCKS, 128), f32)
    scalar = jax.ShapeDtypeStruct((BLOCKS, 128), f32)
    outs = [exchange, exchange]
    if mode == "F" and not first:
        outs += [vector, vector]
    if mode == "FJ":
        outs += [vector, vector, scalar]
    if mode == "J":
        outs += [vector, vector, scalar] + ([vector] if first else [])
    vmem = pl.BlockSpec(memory_space=pltpu.VMEM)
    smem = pl.BlockSpec(memory_space=pltpu.SMEM)
    return pl.pallas_call(
        functools.partial(sweep_kernel, mode, first, kick),
        out_shape=outs,
        in_specs=[smem, smem] + [vmem] * len(arrays),
        out_specs=[vmem] * len(outs),
        scratch_shapes=[
            pltpu.VMEM((BLOCKS, 16, 128), f32),
            pltpu.VMEM((BLOCKS, 128, 128), f32),
            pltpu.VMEM((BLOCKS, 128, 128), f32),
            pltpu.VMEM((made, BLOCKS, 8, 128), f32),
        ],
        compiler_params=pltpu.CompilerParams(vmem_limit_bytes=32 * 1024 * 1024),
        name=f"sweep_{mode}",
    )(plist, total, *arrays)


def exchanged(A, B):
    rA, rB = send(A, swap_pairs(1, 0)), send(B, swap_pairs(1, 1))
    T0, T1 = A + rA, B + rB
    C = jnp.concatenate([T0[:, 0:4], T1[:, 0:4]], axis=1)
    D = jnp.concatenate([T0[:, 4:8], T1[:, 4:8]], axis=1)
    return C, send(C, swap_pairs(0, 0)), D, send(D, swap_pairs(0, 1))


def on_device(
    positions,
    velocities,
    charges,
    atom_types,
    atom_count,
    sigma_type,
    epsilon_type,
    masses,
    pair_list,
    pair_count,
    pos_cotangent,
    vel_cotangent,
):
    f32 = jnp.float32
    a = lax.axis_index("gx")
    y, z = column_of_device()
    y_even, z_even = y % 2 == 0, z % 2 == 0
    counts = atom_count[0, :, 0]
    alive = (lax.broadcasted_iota(jnp.int32, (4, 128), 1) < counts[:, None]).astype(f32)
    kinds = (atom_types[0, :, 0][:, None, :] == lax.broadcasted_iota(jnp.int32, (16, 1), 0)).astype(f32)
    sigma = jnp.sum(kinds * sigma_type[:, None], axis=1)
    epsilon = jnp.sum(kinds * epsilon_type[:, None], axis=1)
    listed = jnp.concatenate(
        [pair_list[0, 0, 0].reshape(112), jnp.broadcast_to(pair_count[0, 0, 0], (16,))]
    ).astype(f32)
    bundle = jnp.concatenate(
        [
            positions[0, :, 0],
            velocities[0, :, 0],
            jnp.stack(
                [charges[0, :, 0] * alive, sigma, jnp.sqrt(epsilon) * alive, 1.0 / masses[0, :, 0]], axis=1
            ),
            pos_cotangent[0, :, 0],
            vel_cotangent[0, :, 0],
            jnp.broadcast_to(counts.astype(f32)[:, None, None], (4, 1, 128)),
            jnp.broadcast_to(listed[None, None, :], (4, 1, 128)),
        ],
        axis=1,
    )
    turned = lax.dynamic_slice_in_dim(jnp.concatenate([bundle, bundle]), a, 4)
    got = [send(turned[t], spread_pairs(t)) for t in range(4)]
    stacked = jnp.stack(got[::-1])
    y_in_four = y % 4
    own = lax.dynamic_slice_in_dim(jnp.concatenate([stacked, stacked]), 3 - y_in_four, 4)
    own = jnp.swapaxes(own, 0, 1)
    lists = own[17].astype(jnp.int32)
    own = own[:17]
    upper = send(own, down_pairs(1))
    wide = jnp.where(
        z_even, jnp.concatenate([upper, own], axis=1), jnp.concatenate([own, upper], axis=1)
    )
    upper = send(wide, down_pairs(0))
    ext = jnp.where(
        y_even, jnp.concatenate([upper, wide], axis=1), jnp.concatenate([wide, upper], axis=1)
    )
    y_role, z_role = jnp.where(y_even, 1, 0), jnp.where(z_even, 1, 0)
    smem = pl.BlockSpec(memory_space=pltpu.SMEM)
    plist, total = pl.pallas_call(
        list_kernel,
        out_shape=[jax.ShapeDtypeStruct((64,), jnp.int32), jax.ShapeDtypeStruct((1,), jnp.int32)],
        in_specs=[smem] * 3,
        out_specs=[smem] * 2,
        name="keep_pairs",
    )(
        lists,
        ext[16, :, 0].astype(jnp.int32),
        jnp.stack([y_in_four, y_role, z_role]).astype(jnp.int32),
    )
    history = [ext[0:3]]
    A, B = sweep("F", True, 0.0, plist, total, [ext])
    x, v = ext[0:3], ext[3:6]
    for step in range(STEPS):
        parts = exchanged(A, B)
        kick = HALF if step == 0 else TIME_STEP
        mode = "F" if step < STEPS - 1 else "FJ"
        A, B, x, v, *rest = sweep(mode, False, kick, plist, total, [ext, x, v, *parts])
        history.append(x)
    charge = rest[0]
    ax, av = ext[10:13], ext[13:16]
    for step in range(STEPS - 1, -1, -1):
        parts = exchanged(A, B)
        first = step == STEPS - 1
        factor = TIME_STEP if step > 0 else HALF
        A, B, ax, av, charge, *rest = sweep(
            "J",
            first,
            factor,
            plist,
            total,
            [ext, history[step], ax, av, *parts, charge] + ([v] if first else []),
        )
        if first:
            v = rest[0]
    sides = charge.reshape(2, 2, 4, 128)
    A = jnp.concatenate([A, sides[:, 0].reshape(1, 8, 128)])
    B = jnp.concatenate([B, sides[:, 1].reshape(1, 8, 128)])
    C, rC, D, rD = exchanged(A, B)
    sums = jnp.concatenate([C + rC, D + rD], axis=1)
    whole = jnp.concatenate([x, v, ax + sums[:3], av, sums[3:4]])
    mine = lax.dynamic_slice_in_dim(whole, (y_role * 2 + z_role) * 4, 4, axis=1)
    mine = jnp.swapaxes(mine, 0, 1)
    turned = lax.dynamic_slice_in_dim(jnp.concatenate([mine, mine]), (y_in_four + 1) % 4, 4)
    got = [send(turned[3 - t], [(q, p) for p, q in spread_pairs(t)]) for t in range(4)]
    stacked = jnp.stack(got)
    out = lax.dynamic_slice_in_dim(jnp.concatenate([stacked, stacked]), (4 - a) % 4, 4)
    out = out[None, :, None]
    return (
        out[:, :, :, 0:3],
        out[:, :, :, 3:6],
        out[:, :, :, 6:9],
        out[:, :, :, 9:12],
        out[:, :, :, 12] * alive[None, :, None],
    )


def solution(mesh):
    vector = P("gx", "gy", "gz", None, None)
    scalar = P("gx", "gy", "gz", None)
    block = P("gx", "gy", "gz")
    in_specs = (
        vector, vector, scalar, scalar, block, P(), P(), scalar, vector, block, vector, vector,
    )
    out_specs = (vector, vector, vector, vector, scalar)
    return jax.shard_map(on_device, mesh=mesh, in_specs=in_specs, out_specs=out_specs, check_vma=False)
```

time: 1000 us -> 494 us (0.49); the launches traced: 982 us -> 497 us
  other arithmetic: 419 us -> 3.14 us
  local copies, waits for them, and re-layouts: 155 us -> 7.68 us
  starting transfers between devices: 216 us -> 312 us
  Pallas kernels: 0 us -> 86.4 us
  waiting for transfers between devices: 160 us -> 85.9 us
  matrix products: 17.1 us -> 0 us
  loops' own time: 11.7 us -> 0 us
    add_any x48 -> x0, other arithmetic: 206 us -> none  [tile_energy(): fraction = squared_sigma / (distance + squared_sigma)]
    reduce_sum x121 -> x1, other arithmetic: 191 us -> 0.09 us  [on_device(): epsilon = jnp.sum(kinds * epsilon_type[:, None], axis=1)]
    gather x240 -> x0, local copies, waits for them, and re-layouts: 140 us -> none  [the longest x48 28.1 us: pair_terms(): right_par = jnp.take(flat_par, second_ids, axis=0)]
    ppermute x72 -> x54, starting transfers between devices: 216 us -> 312 us  [send(): return lax.ppermute(value, AXES, pairs)]
    pallas_call x0 -> x12, Pallas kernels: none -> 86.4 us  [the longest x11 83.4 us: sweep(): pl.pallas_call(functools.partial(sweep_kernel, mode, first, kick), out_sh...]
    ppermute x72 -> x54, waiting for transfers between devices: 160 us -> 85.9 us  [send(): return lax.ppermute(value, AXES, pairs)]
    dot_general x96 -> x0, matrix products: 17.1 us -> none  [the longest x48 8.56 us: one_batch(): jnp.dot(left_select, left_rows.reshape(group, rows_total * per_block), pr...]
    another operation x12 -> x0, loops' own time: 11.7 us -> none  [sweep(): totals = lax.fori_loop(0, rounds, one_batch, initial)]
  transfers between devices with their start and end apart: 72 -> 54, of which waited for: 62 -> 28; matrix products, arithmetic and copies ran while one was open for 10% -> 0% of each run, Pallas kernels for 0% -> 0%
where the time goes in v1:
time: 494 us; the launch traced here: 497 us
  starting transfers between devices  312 us (63%)
  Pallas kernels  86.4 us (17%)
  waiting for transfers between devices  85.9 us (17%)
  local copies, waits for them, and re-layouts  7.68 us (2%)
    ppermute x54, starting transfers between devices, send(): return lax.ppermute(value, AXES, pairs)  312 us
    ppermute x54, waiting for transfers between devices, send(): return lax.ppermute(value, AXES, pairs)  85.9 us
    pallas_call x11, Pallas kernels, sweep(): pl.pallas_call(functools.partial(sweep_kernel, mode, first, kick), out_sh...  83.4 us
  transfers between devices with their start and end apart: 54, of which 28 were waited for; matrix products, arithmetic and copies ran while one was open for 0% of the time, Pallas kernels for 0%

profile of v1, /device:TPU:96, one launch (start us, length us, event | category | flops | bytes accessed | tf_op | source)
XLA Modules:
  0.0 497.1 jit_solution(12661390120009502365)
XLA Ops:
  5.8 5.6 %collective-permute-start.2 = (f32[18,128]{1,0:T(8,128)S(1)}, f32[18,128]{1,0:T(8,128)S(1)}, u32[]{:S(2)}, u32[]{:S(2)}) collective-permute-start(f32[18,128]{1,0:T(8,128)S(1)} %get-tuple-element.129), channel_id=1, source_target_pairs={{0,1},{1,17},{2,49},{3,33},{4,5},{5,21},{6,53},{7,37},{8,9},{9,25}... | collective-permute-start | bytes 27656 | tf_op jit(solution)/shard_map/ppermute | solution.py:74
  45.4 7.1 %sweep_F.5 = (f32[3,8,128]{2,1,0:T(8,128)S(1)}, f32[3,8,128]{2,1,0:T(8,128)S(1)}) custom-call(s32[64]{0:T(128)S(1)} %copy-done, s32[1]{0:T(128)} %get-tuple-element.57.total_ref, f32[17,16,128]{2,1,0:T(8,128)S(1)} %maximum_select_fusion.refs_0_), custom_call_target="tpu_custom_call" | custom-call | tf_op jit(solution)/shard_map/sweep_F/pallas_call | solution.py:297
  52.5 7.4 %collective-permute-start.6 = (f32[3,8,128]{2,1,0:T(8,128)S(1)}, f32[3,8,128]{2,1,0:T(8,128)S(1)}, u32[]{:S(2)}, u32[]{:S(2)}) collective-permute-start(f32[3,8,128]{2,1,0:T(8,128)S(1)} %get-tuple-element.58), channel_id=1, source_target_pairs={{0,16},{16,0},{48,32},{32,48},{4,20},{20,4},{52,36},{36,52},{8,24}... | collective-permute-start | bytes 36872 | tf_op jit(solution)/shard_map/ppermute | solution.py:74
  73.0 7.1 %sweep_F.6 = (f32[3,8,128]{2,1,0:T(8,128)S(1)}, f32[3,8,128]{2,1,0:T(8,128)S(1)}, f32[3,16,128]{2,1,0:T(8,128)S(1)}, f32[3,16,128]{2,1,0:T(8,128)S(1)}) custom-call(s32[64]{0:T(128)S(1)} %copy-done, s32[1]{0:T(128)} %get-tuple-element.57.total_ref, f32[17,16,128]{2,1,0:T(8,128)S(1)} %maximum_select_fusion.refs_0_, ...), custom_call_target="tpu_custom_call" | custom-call | tf_op jit(solution)/shard_map/sweep_F/pallas_call | solution.py:297
  80.2 13.4 %collective-permute-start.10 = (f32[3,8,128]{2,1,0:T(8,128)S(1)}, f32[3,8,128]{2,1,0:T(8,128)S(1)}, u32[]{:S(2)}, u32[]{:S(2)}) collective-permute-start(f32[3,8,128]{2,1,0:T(8,128)S(1)} %get-tuple-element.62), channel_id=1, source_target_pairs={{0,16},{16,0},{48,32},{32,48},{4,20},{20,4},{52,36},{36,52},{8,24}... | collective-permute-start | bytes 36872 | tf_op jit(solution)/shard_map/ppermute | solution.py:74
  107.4 7.1 %sweep_F.7 = (f32[3,8,128]{2,1,0:T(8,128)S(1)}, f32[3,8,128]{2,1,0:T(8,128)S(1)}, f32[3,16,128]{2,1,0:T(8,128)S(1)}, f32[3,16,128]{2,1,0:T(8,128)S(1)}) custom-call(s32[64]{0:T(128)S(1)} %copy-done, s32[1]{0:T(128)} %get-tuple-element.57.total_ref, f32[17,16,128]{2,1,0:T(8,128)S(1)} %maximum_select_fusion.refs_0_, ...), custom_call_target="tpu_custom_call" | custom-call | tf_op jit(solution)/shard_map/sweep_F/pallas_call | solution.py:297
  114.6 16.5 %collective-permute-start.14 = (f32[3,8,128]{2,1,0:T(8,128)S(1)}, f32[3,8,128]{2,1,0:T(8,128)S(1)}, u32[]{:S(2)}, u32[]{:S(2)}) collective-permute-start(f32[3,8,128]{2,1,0:T(8,128)S(1)} %get-tuple-element.66), channel_id=1, source_target_pairs={{0,16},{16,0},{48,32},{32,48},{4,20},{20,4},{52,36},{36,52},{8,24}... | collective-permute-start | bytes 36872 | tf_op jit(solution)/shard_map/ppermute | solution.py:74
  142.9 7.1 %sweep_F.8 = (f32[3,8,128]{2,1,0:T(8,128)S(1)}, f32[3,8,128]{2,1,0:T(8,128)S(1)}, f32[3,16,128]{2,1,0:T(8,128)S(1)}, f32[3,16,128]{2,1,0:T(8,128)S(1)}) custom-call(s32[64]{0:T(128)S(1)} %copy-done, s32[1]{0:T(128)} %get-tuple-element.57.total_ref, f32[17,16,128]{2,1,0:T(8,128)S(1)} %maximum_select_fusion.refs_0_, ...), custom_call_target="tpu_custom_call" | custom-call | tf_op jit(solution)/shard_map/sweep_F/pallas_call | solution.py:297
  150.1 18.5 %collective-permute-start.18 = (f32[3,8,128]{2,1,0:T(8,128)S(1)}, f32[3,8,128]{2,1,0:T(8,128)S(1)}, u32[]{:S(2)}, u32[]{:S(2)}) collective-permute-start(f32[3,8,128]{2,1,0:T(8,128)S(1)} %get-tuple-element.70), channel_id=1, source_target_pairs={{0,16},{16,0},{48,32},{32,48},{4,20},{20,4},{52,36},{36,52},{8,24}... | collective-permute-start | bytes 36872 | tf_op jit(solution)/shard_map/ppermute | solution.py:74
  179.2 7.1 %sweep_F.9 = (f32[3,8,128]{2,1,0:T(8,128)S(1)}, f32[3,8,128]{2,1,0:T(8,128)S(1)}, f32[3,16,128]{2,1,0:T(8,128)S(1)}, f32[3,16,128]{2,1,0:T(8,128)S(1)}) custom-call(s32[64]{0:T(128)S(1)} %copy-done, s32[1]{0:T(128)} %get-tuple-element.57.total_ref, f32[17,16,128]{2,1,0:T(8,128)S(1)} %maximum_select_fusion.refs_0_, ...), custom_call_target="tpu_custom_call" | custom-call | tf_op jit(solution)/shard_map/sweep_F/pallas_call | solution.py:297
  186.4 19.7 %collective-permute-start.22 = (f32[3,8,128]{2,1,0:T(8,128)S(1)}, f32[3,8,128]{2,1,0:T(8,128)S(1)}, u32[]{:S(2)}, u32[]{:S(2)}) collective-permute-start(f32[3,8,128]{2,1,0:T(8,128)S(1)} %get-tuple-element.74), channel_id=1, source_target_pairs={{0,16},{16,0},{48,32},{32,48},{4,20},{20,4},{52,36},{36,52},{8,24}... | collective-permute-start | bytes 36872 | tf_op jit(solution)/shard_map/ppermute | solution.py:74
  216.8 7.9 %sweep_FJ.1 = (f32[6,8,128]{2,1,0:T(8,128)S(1)}, f32[6,8,128]{2,1,0:T(8,128)S(1)}, f32[3,16,128]{2,1,0:T(8,128)S(1)}, f32[3,16,128]{2,1,0:T(8,128)S(1)}, f32[16,128]{1,0:T(8,128)S(1)}) custom-call(s32[64]{0:T(128)S(1)} %copy-done, s32[1]{0:T(128)} %get-tuple-element.57.total_ref, f32[17,16,128]{2,1,0:T(8,128)S(1)} %maximum_select_fusion.refs_0_, ...), custom_call_target="tpu_custom_call" | custom-call | tf_op jit(solution)/shard_map/sweep_FJ/pallas_call | solution.py:297
  224.7 21.4 %collective-permute-start.26 = (f32[6,8,128]{2,1,0:T(8,128)S(1)}, f32[6,8,128]{2,1,0:T(8,128)S(1)}, u32[]{:S(2)}, u32[]{:S(2)}) collective-permute-start(f32[6,8,128]{2,1,0:T(8,128)S(1)} %get-tuple-element.77), channel_id=1, source_target_pairs={{0,16},{16,0},{48,32},{32,48},{4,20},{20,4},{52,36},{36,52},{8,24}... | collective-permute-start | bytes 73736 | tf_op jit(solution)/shard_map/ppermute | solution.py:74
  256.9 8.0 %sweep_J.5 = (f32[3,8,128]{2,1,0:T(8,128)S(1)}, f32[3,8,128]{2,1,0:T(8,128)S(1)}, f32[3,16,128]{2,1,0:T(8,128)S(1)}, f32[3,16,128]{2,1,0:T(8,128)S(1)}, f32[16,1...) custom-call(s32[64]{0:T(128)S(1)} %copy-done, s32[1]{0:T(128)} %get-tuple-element.57.total_ref, ...), custom_call_target="tpu_custom_call" | custom-call | tf_op jit(solution)/shard_map/sweep_J/pallas_call | solution.py:297
  264.9 22.6 %collective-permute-start.30 = (f32[3,8,128]{2,1,0:T(8,128)S(1)}, f32[3,8,128]{2,1,0:T(8,128)S(1)}, u32[]{:S(2)}, u32[]{:S(2)}) collective-permute-start(f32[3,8,128]{2,1,0:T(8,128)S(1)} %get-tuple-element.84), channel_id=1, source_target_pairs={{0,16},{16,0},{48,32},{32,48},{4,20},{20,4},{52,36},{36,52},{8,24}... | collective-permute-start | bytes 36872 | tf_op jit(solution)/shard_map/ppermute | solution.py:74
  298.1 7.9 %sweep_J.6 = (f32[3,8,128]{2,1,0:T(8,128)S(1)}, f32[3,8,128]{2,1,0:T(8,128)S(1)}, f32[3,16,128]{2,1,0:T(8,128)S(1)}, f32[3,16,128]{2,1,0:T(8,128)S(1)}, f32[16,128]{1,0:T(8,128)S(1)}) custom-call(s32[64]{0:T(128)S(1)} %copy-done, s32[1]{0:T(128)} %get-tuple-element.57.total_ref, f32[17,16,128]{2,1,0:T(8,128)S(1)} %maximum_select_fusion.refs_0_, ...), custom_call_target="tpu_custom_call" | custom-call | tf_op jit(solution)/shard_map/sweep_J/pallas_call | solution.py:297
  306.0 22.6 %collective-permute-start.34 = (f32[3,8,128]{2,1,0:T(8,128)S(1)}, f32[3,8,128]{2,1,0:T(8,128)S(1)}, u32[]{:S(2)}, u32[]{:S(2)}) collective-permute-start(f32[3,8,128]{2,1,0:T(8,128)S(1)} %get-tuple-element.89), channel_id=1, source_target_pairs={{0,16},{16,0},{48,32},{32,48},{4,20},{20,4},{52,36},{36,52},{8,24}... | collective-permute-start | bytes 36872 | tf_op jit(solution)/shard_map/ppermute | solution.py:74
  339.3 7.9 %sweep_J.7 = (f32[3,8,128]{2,1,0:T(8,128)S(1)}, f32[3,8,128]{2,1,0:T(8,128)S(1)}, f32[3,16,128]{2,1,0:T(8,128)S(1)}, f32[3,16,128]{2,1,0:T(8,128)S(1)}, f32[16,128]{1,0:T(8,128)S(1)}) custom-call(s32[64]{0:T(128)S(1)} %copy-done, s32[1]{0:T(128)} %get-tuple-element.57.total_ref, f32[17,16,128]{2,1,0:T(8,128)S(1)} %maximum_select_fusion.refs_0_, ...), custom_call_target="tpu_custom_call" | custom-call | tf_op jit(solution)/shard_map/sweep_J/pallas_call | solution.py:297
  347.2 22.6 %collective-permute-start.38 = (f32[3,8,128]{2,1,0:T(8,128)S(1)}, f32[3,8,128]{2,1,0:T(8,128)S(1)}, u32[]{:S(2)}, u32[]{:S(2)}) collective-permute-start(f32[3,8,128]{2,1,0:T(8,128)S(1)} %get-tuple-element.94), channel_id=1, source_target_pairs={{0,16},{16,0},{48,32},{32,48},{4,20},{20,4},{52,36},{36,52},{8,24}... | collective-permute-start | bytes 36872 | tf_op jit(solution)/shard_map/ppermute | solution.py:74
  380.4 7.9 %sweep_J.8 = (f32[3,8,128]{2,1,0:T(8,128)S(1)}, f32[3,8,128]{2,1,0:T(8,128)S(1)}, f32[3,16,128]{2,1,0:T(8,128)S(1)}, f32[3,16,128]{2,1,0:T(8,128)S(1)}, f32[16,128]{1,0:T(8,128)S(1)}) custom-call(s32[64]{0:T(128)S(1)} %copy-done, s32[1]{0:T(128)} %get-tuple-element.57.total_ref, f32[17,16,128]{2,1,0:T(8,128)S(1)} %maximum_select_fusion.refs_0_, ...), custom_call_target="tpu_custom_call" | custom-call | tf_op jit(solution)/shard_map/sweep_J/pallas_call | solution.py:297
  388.3 22.6 %collective-permute-start.42 = (f32[3,8,128]{2,1,0:T(8,128)S(1)}, f32[3,8,128]{2,1,0:T(8,128)S(1)}, u32[]{:S(2)}, u32[]{:S(2)}) collective-permute-start(f32[3,8,128]{2,1,0:T(8,128)S(1)} %get-tuple-element.99), channel_id=1, source_target_pairs={{0,16},{16,0},{48,32},{32,48},{4,20},{20,4},{52,36},{36,52},{8,24}... | collective-permute-start | bytes 36872 | tf_op jit(solution)/shard_map/ppermute | solution.py:74
  421.5 7.9 %sweep_J.9 = (f32[3,8,128]{2,1,0:T(8,128)S(1)}, f32[3,8,128]{2,1,0:T(8,128)S(1)}, f32[3,16,128]{2,1,0:T(8,128)S(1)}, f32[3,16,128]{2,1,0:T(8,128)S(1)}, f32[16,128]{1,0:T(8,128)S(1)}) custom-call(s32[64]{0:T(128)S(1)} %copy-done, s32[1]{0:T(128)} %get-tuple-element.57.total_ref, f32[17,16,128]{2,1,0:T(8,128)S(1)} %maximum_select_fusion.refs_0_, ...), custom_call_target="tpu_custom_call" | custom-call | tf_op jit(solution)/shard_map/sweep_J/pallas_call | solution.py:297
  429.5 22.6 %collective-permute-start.46 = (f32[4,8,128]{2,1,0:T(8,128)S(1)}, f32[4,8,128]{2,1,0:T(8,128)S(1)}, u32[]{:S(2)}, u32[]{:S(2)}) collective-permute-start(f32[4,8,128]{2,1,0:T(8,128)S(1)} %pad_maximum_fusion.2), channel_id=1, source_target_pairs={{0,16},{16,0},{48,32},{32,48},{4,20},{20,4},{52,36},{36,52},{8,24}... | collective-permute-start | bytes 49160 | tf_op jit(solution)/shard_map/ppermute | solution.py:74
  462.9 18.2 %collective-permute-start.50 = (f32[13,128]{1,0:T(8,128)S(1)}, f32[13,128]{1,0:T(8,128)S(1)}, u32[]{:S(2)}, u32[]{:S(2)}) collective-permute-start(f32[13,128]{1,0:T(8,128)S(1)} %bitcast.91), channel_id=1, source_target_pairs={{0,0},{16,1},{48,2},{32,3},{4,4},{20,5},{52,6},{36,7},{8,8},{24,9}... | collective-permute-start | bytes 19976 | tf_op jit(solution)/shard_map/ppermute | solution.py:74
  (246 shorter events, 177.7 us)
Async XLA Ops:
  5.8 16.2 %collective-permute-start.2 = (f32[18,128]{1,0:T(8,128)S(1)}, f32[18,128]{1,0:T(8,128)S(1)}, u32[]{:S(2)}, u32[]{:S(2)}) collective-permute-start(f32[18,128]{1,0:T(8,128)S(1)} %get-tuple-element.129), channel_id=1, source_target_pairs={{0,1},{1,17},{2,49},{3,33},{4,5},{5,21},{6,53},{7,37},{8,9},{9,25}... | collective-permute-start | bytes 27656 | tf_op jit(solution)/shard_map/ppermute | solution.py:74
  11.4 10.6 %collective-permute-start.1 = (f32[18,128]{1,0:T(8,128)S(1)}, f32[18,128]{1,0:T(8,128)S(1)}, u32[]{:S(2)}, u32[]{:S(2)}) collective-permute-start(f32[18,128]{1,0:T(8,128)S(1)} %get-tuple-element.130), channel_id=1, source_target_pairs={{0,2},{1,18},{2,50},{3,34},{4,6},{5,22},{6,54},{7,38},{8,10},{9,26... | collective-permute-start | bytes 27656 | tf_op jit(solution)/shard_map/ppermute | solution.py:74
  19.9 7.7 %collective-permute-start.3 = (f32[18,128]{1,0:T(8,128)S(1)}, f32[18,128]{1,0:T(8,128)S(1)}, u32[]{:S(2)}, u32[]{:S(2)}) collective-permute-start(f32[18,128]{1,0:T(8,128)S(1)} %get-tuple-element.128), channel_id=1, source_target_pairs={{0,0},{1,16},{2,48},{3,32},{4,4},{5,20},{6,52},{7,36},{8,8},{9,24}... | collective-permute-start | bytes 27656 | tf_op jit(solution)/shard_map/ppermute | solution.py:74
  27.8 7.0 %collective-permute-start.4 = (f32[17,4,128]{2,1,0:T(4,128)S(1)}, f32[17,4,128]{2,1,0:T(4,128)S(1)}, u32[]{:S(2)}, u32[]{:S(2)}) collective-permute-start(f32[17,4,128]{2,1,0:T(4,128)S(1)} %slice.278), channel_id=1, source_target_pairs={{16,0},{48,16},{32,48},{4,32},{20,4},{52,20},{36,52},{8,36},{24,8}... | collective-permute-start | bytes 104456 | tf_op jit(solution)/shard_map/ppermute | solution.py:74
  52.5 11.6 %collective-permute-start.6 = (f32[3,8,128]{2,1,0:T(8,128)S(1)}, f32[3,8,128]{2,1,0:T(8,128)S(1)}, u32[]{:S(2)}, u32[]{:S(2)}) collective-permute-start(f32[3,8,128]{2,1,0:T(8,128)S(1)} %get-tuple-element.58), channel_id=1, source_target_pairs={{0,16},{16,0},{48,32},{32,48},{4,20},{20,4},{52,36},{36,52},{8,24}... | collective-permute-start | bytes 36872 | tf_op jit(solution)/shard_map/ppermute | solution.py:74
  80.2 15.3 %collective-permute-start.10 = (f32[3,8,128]{2,1,0:T(8,128)S(1)}, f32[3,8,128]{2,1,0:T(8,128)S(1)}, u32[]{:S(2)}, u32[]{:S(2)}) collective-permute-start(f32[3,8,128]{2,1,0:T(8,128)S(1)} %get-tuple-element.62), channel_id=1, source_target_pairs={{0,16},{16,0},{48,32},{32,48},{4,20},{20,4},{52,36},{36,52},{8,24}... | collective-permute-start | bytes 36872 | tf_op jit(solution)/shard_map/ppermute | solution.py:74
  100.3 7.1 %collective-permute-start.12 = (f32[3,8,128]{2,1,0:T(8,128)S(1)}, f32[3,8,128]{2,1,0:T(8,128)S(1)}, u32[]{:S(2)}, u32[]{:S(2)}) collective-permute-start(f32[3,8,128]{2,1,0:T(8,128)S(1)} %pad_maximum_fusion.8.refs_3_), channel_id=1, source_target_pairs={{0,1},{16,17},{48,49},{32,33},{4,5},{20,21},{52,53},{36,37},{8,9},... | collective-permute-start | bytes 36872 | tf_op jit(solution)/shard_map/ppermute | solution.py:74
  114.6 18.4 %collective-permute-start.14 = (f32[3,8,128]{2,1,0:T(8,128)S(1)}, f32[3,8,128]{2,1,0:T(8,128)S(1)}, u32[]{:S(2)}, u32[]{:S(2)}) collective-permute-start(f32[3,8,128]{2,1,0:T(8,128)S(1)} %get-tuple-element.66), channel_id=1, source_target_pairs={{0,16},{16,0},{48,32},{32,48},{4,20},{20,4},{52,36},{36,52},{8,24}... | collective-permute-start | bytes 36872 | tf_op jit(solution)/shard_map/ppermute | solution.py:74
  131.1 6.8 %collective-permute-start.15 = (f32[3,8,128]{2,1,0:T(8,128)S(1)}, f32[3,8,128]{2,1,0:T(8,128)S(1)}, u32[]{:S(2)}, u32[]{:S(2)}) collective-permute-start(f32[3,8,128]{2,1,0:T(8,128)S(1)} %get-tuple-element.67), channel_id=1, source_target_pairs={{16,48},{48,16},{32,4},{4,32},{20,52},{52,20},{36,8},{8,36},{24,56... | collective-permute-start | bytes 36872 | tf_op jit(solution)/shard_map/ppermute | solution.py:74
  150.1 20.4 %collective-permute-start.18 = (f32[3,8,128]{2,1,0:T(8,128)S(1)}, f32[3,8,128]{2,1,0:T(8,128)S(1)}, u32[]{:S(2)}, u32[]{:S(2)}) collective-permute-start(f32[3,8,128]{2,1,0:T(8,128)S(1)} %get-tuple-element.70), channel_id=1, source_target_pairs={{0,16},{16,0},{48,32},{32,48},{4,20},{20,4},{52,36},{36,52},{8,24}... | collective-permute-start | bytes 36872 | tf_op jit(solution)/shard_map/ppermute | solution.py:74
  186.4 21.7 %collective-permute-start.22 = (f32[3,8,128]{2,1,0:T(8,128)S(1)}, f32[3,8,128]{2,1,0:T(8,128)S(1)}, u32[]{:S(2)}, u32[]{:S(2)}) collective-permute-start(f32[3,8,128]{2,1,0:T(8,128)S(1)} %get-tuple-element.74), channel_id=1, source_target_pairs={{0,16},{16,0},{48,32},{32,48},{4,20},{20,4},{52,36},{36,52},{8,24}... | collective-permute-start | bytes 36872 | tf_op jit(solution)/shard_map/ppermute | solution.py:74
  206.1 6.8 %collective-permute-start.23 = (f32[3,8,128]{2,1,0:T(8,128)S(1)}, f32[3,8,128]{2,1,0:T(8,128)S(1)}, u32[]{:S(2)}, u32[]{:S(2)}) collective-permute-start(f32[3,8,128]{2,1,0:T(8,128)S(1)} %get-tuple-element.75), channel_id=1, source_target_pairs={{16,48},{48,16},{32,4},{4,32},{20,52},{52,20},{36,8},{8,36},{24,56... | collective-permute-start | bytes 36872 | tf_op jit(solution)/shard_map/ppermute | solution.py:74
  224.7 23.3 %collective-permute-start.26 = (f32[6,8,128]{2,1,0:T(8,128)S(1)}, f32[6,8,128]{2,1,0:T(8,128)S(1)}, u32[]{:S(2)}, u32[]{:S(2)}) collective-permute-start(f32[6,8,128]{2,1,0:T(8,128)S(1)} %get-tuple-element.77), channel_id=1, source_target_pairs={{0,16},{16,0},{48,32},{32,48},{4,20},{20,4},{52,36},{36,52},{8,24}... | collective-permute-start | bytes 73736 | tf_op jit(solution)/shard_map/ppermute | solution.py:74
  246.1 6.9 %collective-permute-start.27 = (f32[6,8,128]{2,1,0:T(8,128)S(1)}, f32[6,8,128]{2,1,0:T(8,128)S(1)}, u32[]{:S(2)}, u32[]{:S(2)}) collective-permute-start(f32[6,8,128]{2,1,0:T(8,128)S(1)} %get-tuple-element.78), channel_id=1, source_target_pairs={{16,48},{48,16},{32,4},{4,32},{20,52},{52,20},{36,8},{8,36},{24,56... | collective-permute-start | bytes 73736 | tf_op jit(solution)/shard_map/ppermute | solution.py:74
  264.9 24.5 %collective-permute-start.30 = (f32[3,8,128]{2,1,0:T(8,128)S(1)}, f32[3,8,128]{2,1,0:T(8,128)S(1)}, u32[]{:S(2)}, u32[]{:S(2)}) collective-permute-start(f32[3,8,128]{2,1,0:T(8,128)S(1)} %get-tuple-element.84), channel_id=1, source_target_pairs={{0,16},{16,0},{48,32},{32,48},{4,20},{20,4},{52,36},{36,52},{8,24}... | collective-permute-start | bytes 36872 | tf_op jit(solution)/shard_map/ppermute | solution.py:74
  306.0 24.5 %collective-permute-start.34 = (f32[3,8,128]{2,1,0:T(8,128)S(1)}, f32[3,8,128]{2,1,0:T(8,128)S(1)}, u32[]{:S(2)}, u32[]{:S(2)}) collective-permute-start(f32[3,8,128]{2,1,0:T(8,128)S(1)} %get-tuple-element.89), channel_id=1, source_target_pairs={{0,16},{16,0},{48,32},{32,48},{4,20},{20,4},{52,36},{36,52},{8,24}... | collective-permute-start | bytes 36872 | tf_op jit(solution)/shard_map/ppermute | solution.py:74
  347.2 24.5 %collective-permute-start.38 = (f32[3,8,128]{2,1,0:T(8,128)S(1)}, f32[3,8,128]{2,1,0:T(8,128)S(1)}, u32[]{:S(2)}, u32[]{:S(2)}) collective-permute-start(f32[3,8,128]{2,1,0:T(8,128)S(1)} %get-tuple-element.94), channel_id=1, source_target_pairs={{0,16},{16,0},{48,32},{32,48},{4,20},{20,4},{52,36},{36,52},{8,24}... | collective-permute-start | bytes 36872 | tf_op jit(solution)/shard_map/ppermute | solution.py:74
  388.3 24.5 %collective-permute-start.42 = (f32[3,8,128]{2,1,0:T(8,128)S(1)}, f32[3,8,128]{2,1,0:T(8,128)S(1)}, u32[]{:S(2)}, u32[]{:S(2)}) collective-permute-start(f32[3,8,128]{2,1,0:T(8,128)S(1)} %get-tuple-element.99), channel_id=1, source_target_pairs={{0,16},{16,0},{48,32},{32,48},{4,20},{20,4},{52,36},{36,52},{8,24}... | collective-permute-start | bytes 36872 | tf_op jit(solution)/shard_map/ppermute | solution.py:74
  429.5 24.5 %collective-permute-start.46 = (f32[4,8,128]{2,1,0:T(8,128)S(1)}, f32[4,8,128]{2,1,0:T(8,128)S(1)}, u32[]{:S(2)}, u32[]{:S(2)}) collective-permute-start(f32[4,8,128]{2,1,0:T(8,128)S(1)} %pad_maximum_fusion.2), channel_id=1, source_target_pairs={{0,16},{16,0},{48,32},{32,48},{4,20},{20,4},{52,36},{36,52},{8,24}... | collective-permute-start | bytes 49160 | tf_op jit(solution)/shard_map/ppermute | solution.py:74
  452.1 6.8 %collective-permute-start.47 = (f32[4,8,128]{2,1,0:T(8,128)S(1)}, f32[4,8,128]{2,1,0:T(8,128)S(1)}, u32[]{:S(2)}, u32[]{:S(2)}) collective-permute-start(f32[4,8,128]{2,1,0:T(8,128)S(1)} %pad_maximum_fusion.3), channel_id=1, source_target_pairs={{16,48},{48,16},{32,4},{4,32},{20,52},{52,20},{36,8},{8,36},{24,56... | collective-permute-start | bytes 49160 | tf_op jit(solution)/shard_map/ppermute | solution.py:74
  462.9 22.7 %collective-permute-start.50 = (f32[13,128]{1,0:T(8,128)S(1)}, f32[13,128]{1,0:T(8,128)S(1)}, u32[]{:S(2)}, u32[]{:S(2)}) collective-permute-start(f32[13,128]{1,0:T(8,128)S(1)} %bitcast.91), channel_id=1, source_target_pairs={{0,0},{16,1},{48,2},{32,3},{4,4},{20,5},{52,6},{36,7},{8,8},{24,9}... | collective-permute-start | bytes 19976 | tf_op jit(solution)/shard_map/ppermute | solution.py:74
  481.2 8.8 %collective-permute-start.51 = (f32[13,128]{1,0:T(8,128)S(1)}, f32[13,128]{1,0:T(8,128)S(1)}, u32[]{:S(2)}, u32[]{:S(2)}) collective-permute-start(f32[13,128]{1,0:T(8,128)S(1)} %bitcast.94), channel_id=1, source_target_pairs={{1,0},{17,1},{49,2},{33,3},{5,4},{21,5},{53,6},{37,7},{9,8},{25,9}... | collective-permute-start | bytes 19976 | tf_op jit(solution)/shard_map/ppermute | solution.py:74
  483.6 10.4 %collective-permute-start.52 = (f32[13,128]{1,0:T(8,128)S(1)}, f32[13,128]{1,0:T(8,128)S(1)}, u32[]{:S(2)}, u32[]{:S(2)}) collective-permute-start(f32[13,128]{1,0:T(8,128)S(1)} %bitcast.93), channel_id=1, source_target_pairs={{2,0},{18,1},{50,2},{34,3},{6,4},{22,5},{54,6},{38,7},{10,8},{26,9... | collective-permute-start | bytes 19976 | tf_op jit(solution)/shard_map/ppermute | solution.py:74
  485.5 8.4 %collective-permute-start.53 = (f32[13,128]{1,0:T(8,128)S(1)}, f32[13,128]{1,0:T(8,128)S(1)}, u32[]{:S(2)}, u32[]{:S(2)}) collective-permute-start(f32[13,128]{1,0:T(8,128)S(1)} %bitcast.92), channel_id=1, source_target_pairs={{3,0},{19,1},{51,2},{35,3},{7,4},{23,5},{55,6},{39,7},{11,8},{27,9... | collective-permute-start | bytes 19976 | tf_op jit(solution)/shard_map/ppermute | solution.py:74
  (42 other events, 130.1 us)

commit v2 on v1

--- a/solution.py
+++ b/solution.py
@@ -19,6 +19,8 @@
 ROWS = 18
 TILES = 4
 GROUP = 8 * TILES
+JOBS = 2
+LIST = 56 * (128 // GROUP) + 16
 
 
 def column_device(y, z):
@@ -98,14 +100,17 @@
             left = jnp.where(swap, two_number, one_number)
             right = jnp.where(swap, one_number, two_number)
             steps = (jnp.minimum(one_count, two_count) + (GROUP - 1)) // GROUP
-            word = left + right * 16 + steps * 256
+            word = left + right * 16 + (jnp.where(left == right, 1, 2) << 18)
             for place in range(3):
-                word = word + ((sign * (first[place] - second[place]) + 1) << (13 + 2 * place))
-            out_ref[total] = word
-            return total + jnp.where(mine, 1, 0)
+                word = word + ((sign * (first[place] - second[place]) + 1) << (12 + 2 * place))
+            for step in range(128 // GROUP):
+                out_ref[total + step] = word + step * 256
+            return total + jnp.where(mine, steps, 0)
 
         total = lax.fori_loop(0, jnp.minimum(list_ref[a, 112], 56), one, total)
-    total_ref[0] = total
+    for job in range(JOBS):
+        out_ref[total + job] = 0
+    total_ref[0] = (total + JOBS - 1) // JOBS
 
 
 def inverse_of(value):
@@ -116,16 +121,14 @@
 def sweep_tiles(mode, list_ref, total_ref, rows_ref, columns_ref, row_sum_ref, column_sum_ref):
     forces, pulled = "F" in mode, "J" in mode
     made = 3 * forces + 4 * pulled
-    lane = lax.broadcasted_iota(jnp.int32, (8, 128), 1)
-
-    def one_pair(k, carry):
-        word = list_ref[k]
-        left, right, steps = word & 15, (word >> 4) & 15, (word >> 8) & 31
-        offset = [(((word >> (13 + 2 * c)) & 3) - 1).astype(jnp.float32) for c in range(3)]
-        weight = jnp.where(left == right, 0.5, 1.0).astype(jnp.float32)
+
+    def one_job(word):
+        left, right, step = word & 15, (word >> 4) & 15, (word >> 8) & 15
+        offset = [(((word >> (12 + 2 * c)) & 3) - 1).astype(jnp.float32) for c in range(3)]
+        weight = (word >> 18).astype(jnp.float32) * 0.5
 
         def row(c, scale=None, shift=None):
-            value = rows_ref[right, pl.ds(c, 1), :]
+            value = rows_ref[c, pl.ds(right, 1), :]
             if scale is not None:
                 value = value * scale
             if shift is not None:
@@ -138,70 +141,63 @@
         right_depth = row(5, scale=weight)
         right_cot = [row(6 + c) for c in range(3)] if pulled else None
 
-        def one_step(step, sums):
-            sums = list(sums)
-            for tile in range(TILES):
-                first_row = pl.multiple_of(step * GROUP + 8 * tile, 8)
-                packed = columns_ref[left, pl.ds(first_row, 8), :]
-
-                def column(c):
-                    return jnp.broadcast_to(packed[:, c : c + 1], (8, 128))
-
-                d = [column(c) - right_pos[c] for c in range(3)]
-                charge = column(3)
-                half = column(4) + right_half
-                depth = column(5) * right_depth
-                s = d[0] * d[0] + d[1] * d[1] + d[2] * d[2]
-                sigma2 = half * half
-                r = inverse_of(s + sigma2)
-                t = sigma2 * r
-                p = t * t * t
-                soft = s + SOFT
-                ir = lax.rsqrt(soft)
-                g = jnp.exp((soft * ir) * -KAPPA) * ir
-                fade = jnp.maximum(1.0 - s, 0.0)
-                fade2 = fade * fade
-                fr = fade * r
-                kappa_term = ir + 0.5 * (ir * ir)
-                h = g * (3.0 + fade * kappa_term)
-                dp = depth * p
-                twop = 2.0 * p - 1.0
-                charges = charge * right_charge
-                A = (fade2 * 8.0) * (3.0 * dp * ((p - 1.0) + fr * twop) + charges * h)
-                values = []
-                if forces:
-                    values += [A * d[c] for c in range(3)]
-                if pulled:
-                    w = [column(6 + c) - right_cot[c] for c in range(3)]
-                    dw = d[0] * w[0] + d[1] * w[1] + d[2] * w[2]
-                    ir2 = ir * ir
-                    lj = (6.0 * dp) * ((p - 1.0) + fr * (3.0 * twop + fr * (7.0 * p - 2.0)))
-                    m2 = ir2 * (1.0 + 1.5 * ir + 0.75 * ir2)
-                    cb = (charges * g) * (6.0 + fade * (6.0 * kappa_term + fade * m2))
-                    B = (-16.0 * fade) * (lj + cb) * dw
-                    values += [A * w[c] + B * d[c] for c in range(3)]
-                    common = (8.0 * fade2) * h * dw
-                    values += [common * right_charge]
-                    last = common * charge * weight
-                packed_sum = None
-                for place, value in enumerate(values):
-                    total = jnp.sum(value, axis=1, keepdims=True)
-                    total = jnp.broadcast_to(total, (8, 128))
-                    packed_sum = total if place == 0 else jnp.where(lane == place, total, packed_sum)
-                here = (left, pl.ds(first_row, 8), slice(None))
-                row_sum_ref[here] = row_sum_ref[here] + packed_sum
-                if pulled:
-                    values[-1] = -last
-                sums = [a + b for a, b in zip(sums, values)]
-            return tuple(sums)
-
-        zero = jnp.zeros((8, 128), jnp.float32)
-        sums = lax.fori_loop(0, steps, one_step, (zero,) * made)
+        sums = None
+        for tile in range(TILES):
+            eight = pl.ds(pl.multiple_of(left * 128 + step * GROUP + 8 * tile, 8), 8)
+
+            def column(c):
+                return columns_ref[c, eight, :]
+
+            d = [column(c) - right_pos[c] for c in range(3)]
+            charge = column(3)
+            half = column(4) + right_half
+            depth = column(5) * right_depth
+            s = d[0] * d[0] + d[1] * d[1] + d[2] * d[2]
+            sigma2 = half * half
+            r = inverse_of(s + sigma2)
+            t = sigma2 * r
+            p = t * t * t
+            soft = s + SOFT
+            ir = lax.rsqrt(soft)
+            g = jnp.exp((soft * ir) * -KAPPA) * ir
+            fade = jnp.maximum(1.0 - s, 0.0)
+            fade2 = fade * fade
+            fr = fade * r
+            kappa_term = ir + 0.5 * (ir * ir)
+            h = g * (3.0 + fade * kappa_term)
+            dp = depth * p
+            twop = 2.0 * p - 1.0
+            charges = charge * right_charge
+            A = (fade2 * 8.0) * (3.0 * dp * ((p - 1.0) + fr * twop) + charges * h)
+            values = []
+            if forces:
+                values += [A * d[c] for c in range(3)]
+            if pulled:
+                w = [column(6 + c) - right_cot[c] for c in range(3)]
+                dw = d[0] * w[0] + d[1] * w[1] + d[2] * w[2]
+                ir2 = ir * ir
+                lj = (6.0 * dp) * ((p - 1.0) + fr * (3.0 * twop + fr * (7.0 * p - 2.0)))
+                m2 = ir2 * (1.0 + 1.5 * ir + 0.75 * ir2)
+                cb = (charges * g) * (6.0 + fade * (6.0 * kappa_term + fade * m2))
+                B = (-16.0 * fade) * (lj + cb) * dw
+                values += [A * w[c] + B * d[c] for c in range(3)]
+                common = (8.0 * fade2) * h * dw
+                values += [common * right_charge]
+                last = common * charge * weight
+            for place, value in enumerate(values):
+                row_sum_ref[place, eight, :] = row_sum_ref[place, eight, :] + value
+            if pulled:
+                values[-1] = -last
+            sums = values if sums is None else [a + b for a, b in zip(sums, values)]
         for place in range(made):
             column_sum_ref[place, right] = column_sum_ref[place, right] + sums[place]
+
+    def one_step(k, carry):
+        for job in range(JOBS):
+            one_job(list_ref[k * JOBS + job])
         return carry
 
-    lax.fori_loop(0, total_ref[0], one_pair, jnp.int32(0))
+    lax.fori_loop(0, total_ref[0], one_step, jnp.int32(0))
 
 
 def sweep_kernel(mode, first, kick, list_ref, total_ref, *refs):
@@ -256,31 +252,34 @@
     rows = r["rows"]
     quantities = position + [ext[6], 0.5 * ext[7], ext[8]] + cotangent
     for place, value in enumerate(quantities):
+        rows[place] = value
+        turned = value.T
         for e in range(BLOCKS):
-            rows[e, place : place + 1, :] = value[e : e + 1, :]
-    for e in range(BLOCKS):
-        r["columns"][e, :, 0:16] = rows[e].T
-        r["row_sum"][e] = jnp.zeros((128, 128), jnp.float32)
+            r["columns"][place, e * 128 : (e + 1) * 128, :] = jnp.broadcast_to(turned[:, e : e + 1], (128, 128))
+    r["row_sum"][...] = jnp.zeros(r["row_sum"].shape, jnp.float32)
     r["column_sum"][...] = jnp.zeros(r["column_sum"].shape, jnp.float32)
     sweep_tiles(mode, list_ref, total_ref, rows, r["columns"], r["row_sum"], r["column_sum"])
-    for e in range(BLOCKS):
-        by_row = r["row_sum"][e].T
-        target = r["A"] if (e // 4) % 2 == 0 else r["B"]
-        place = (e // 8) * 4 + e % 4
-        for c in range(made):
-            total = by_row[c : c + 1] - jnp.sum(r["column_sum"][c, e], axis=0, keepdims=True)
-            if pulled and c == made - 1:
-                if mode == "J":
-                    total = total + r["charge"][e : e + 1, :]
-                r["charge_out"][e : e + 1, :] = total
-            else:
-                target[c, place : place + 1, :] = total
+    lane = lax.broadcasted_iota(jnp.int32, (128, BLOCKS), 1)
+    for c in range(made):
+        by_atom = jnp.zeros((128, BLOCKS), jnp.float32)
+        for e in range(BLOCKS):
+            total = jnp.sum(r["row_sum"][c, e * 128 : (e + 1) * 128, :], axis=1, keepdims=True)
+            by_atom = jnp.where(lane == e, jnp.broadcast_to(total, (128, BLOCKS)), by_atom)
+        total = by_atom.T - jnp.sum(r["column_sum"][c], axis=1)
+        if pulled and c == made - 1:
+            if mode == "J":
+                total = total + r["charge"][...]
+            r["charge_out"][...] = total
+        else:
+            r["A"][c] = jnp.concatenate([total[0:4], total[8:12]], axis=0)
+            r["B"][c] = jnp.concatenate([total[4:8], total[12:16]], axis=0)
 
 
 def sweep(mode, first, kick, plist, total, arrays):
     forces, pulled = "F" in mode, "J" in mode
     sent = 3 * forces + 3 * pulled
     made = 3 * forces + 4 * pulled
+    quantities = 6 + 3 * pulled
     f32 = jnp.float32
     exchange = jax.ShapeDtypeStruct((sent, 8, 128), f32)
     vector = jax.ShapeDtypeStruct((3, BLOCKS, 128), f32)
@@ -300,9 +299,9 @@
         in_specs=[smem, smem] + [vmem] * len(arrays),
         out_specs=[vmem] * len(outs),
         scratch_shapes=[
-            pltpu.VMEM((BLOCKS, 16, 128), f32),
-            pltpu.VMEM((BLOCKS, 128, 128), f32),
-            pltpu.VMEM((BLOCKS, 128, 128), f32),
+            pltpu.VMEM((quantities, BLOCKS, 128), f32),
+            pltpu.VMEM((quantities, BLOCKS * 128, 128), f32),
+            pltpu.VMEM((made, BLOCKS * 128, 128), f32),
             pltpu.VMEM((made, BLOCKS, 8, 128), f32),
         ],
         compiler_params=pltpu.CompilerParams(vmem_limit_bytes=32 * 1024 * 1024),
@@ -378,7 +377,7 @@
     smem = pl.BlockSpec(memory_space=pltpu.SMEM)
     plist, total = pl.pallas_call(
         list_kernel,
-        out_shape=[jax.ShapeDtypeStruct((64,), jnp.int32), jax.ShapeDtypeStruct((1,), jnp.int32)],
+        out_shape=[jax.ShapeDtypeStruct((LIST,), jnp.int32), jax.ShapeDtypeStruct((1,), jnp.int32)],
         in_specs=[smem] * 3,
         out_specs=[smem] * 2,
         name="keep_pairs",

time: 494 us -> 348 us (0.70)
  starting transfers between devices: 312 us -> 110 us
  Pallas kernels: 86.4 us -> 138 us
    ppermute x54, starting transfers between devices: 312 us -> 110 us  [send(): return lax.ppermute(value, AXES, pairs)]
    pallas_call x11, Pallas kernels: 83.4 us -> 130 us  [sweep(): pl.pallas_call(functools.partial(sweep_kernel, mode, first, kick), out_sh...]
where the time goes in v2:
time: 348 us; the launch traced here: 349 us
  Pallas kernels  138 us (40%)
  starting transfers between devices  110 us (32%)
  waiting for transfers between devices  87.9 us (25%)
  local copies, waits for them, and re-layouts  7.74 us (2%)
    pallas_call x11, Pallas kernels, sweep(): pl.pallas_call(functools.partial(sweep_kernel, mode, first, kick), out_sh...  130 us
    ppermute x54, starting transfers between devices, send(): return lax.ppermute(value, AXES, pairs)  110 us
    ppermute x54, waiting for transfers between devices, send(): return lax.ppermute(value, AXES, pairs)  87.9 us
    pallas_call x1, Pallas kernels, on_device(): pl.pallas_call(list_kernel, out_shape=[jax.ShapeDtypeStruct((LIST,), jnp....  7.62 us
    unnamed x42, local copies, waits for them, and re-layouts  7.09 us
  transfers between devices with their start and end apart: 54, of which 28 were waited for; matrix products, arithmetic and copies ran while one was open for 0% of the time, Pallas kernels for 0%

profile of v2, /device:TPU:96, one launch (start us, length us, event | category | flops | bytes accessed | tf_op | source)
XLA Modules:
  0.0 349.5 jit_solution(12997825012302955119)
XLA Ops:
  5.8 5.6 %collective-permute-start.2 = (f32[18,128]{1,0:T(8,128)S(1)}, f32[18,128]{1,0:T(8,128)S(1)}, u32[]{:S(2)}, u32[]{:S(2)}) collective-permute-start(f32[18,128]{1,0:T(8,128)S(1)} %get-tuple-element.129), channel_id=1, source_target_pairs={{0,1},{1,17},{2,49},{3,33},{4,5},{5,21},{6,53},{7,37},{8,9},{9,25}... | collective-permute-start | bytes 27656 | tf_op jit(solution)/shard_map/ppermute | solution.py:76
  11.4 5.2 %collective-permute-start.1 = (f32[18,128]{1,0:T(8,128)S(1)}, f32[18,128]{1,0:T(8,128)S(1)}, u32[]{:S(2)}, u32[]{:S(2)}) collective-permute-start(f32[18,128]{1,0:T(8,128)S(1)} %get-tuple-element.130), channel_id=1, source_target_pairs={{0,2},{1,18},{2,50},{3,34},{4,6},{5,22},{6,54},{7,38},{8,10},{9,26... | collective-permute-start | bytes 27656 | tf_op jit(solution)/shard_map/ppermute | solution.py:76
  41.7 7.6 %keep_pairs.1 = (s32[240]{0:T(256)}, s32[1]{0:T(128)}) custom-call(s32[4,128]{1,0:T(4,128)} %fusion.6.list_ref, s32[16]{0:T(128)} %fusion.4.count_ref, s32[3]{0:T(128)} %pad_add_fusion.place_ref), custom_call_target="tpu_custom_call" | custom-call | tf_op jit(solution)/shard_map/keep_pairs/pallas_call | solution.py:378
  50.0 9.2 %sweep_F.5 = (f32[3,8,128]{2,1,0:T(8,128)S(1)}, f32[3,8,128]{2,1,0:T(8,128)S(1)}) custom-call(s32[240]{0:T(256)S(1)} %copy-done, s32[1]{0:T(128)} %get-tuple-element.57.total_ref, f32[17,16,128]{2,1,0:T(8,128)S(1)} %maximum_select_fusion.refs_0_), custom_call_target="tpu_custom_call" | custom-call | tf_op jit(solution)/shard_map/sweep_F/pallas_call | solution.py:296
  61.3 4.8 %collective-permute-done.7 = f32[3,8,128]{2,1,0:T(8,128)S(1)} collective-permute-done((f32[3,8,128]{2,1,0:T(8,128)S(1)}, f32[3,8,128]{2,1,0:T(8,128)S(1)}, u32[]{:S(2)}, u32[]{:S(2)}) %collective-permute-start.7) | collective-permute-done | bytes 12320 | tf_op jit(solution)/shard_map/ppermute | solution.py:76
  69.9 9.2 %sweep_F.6 = (f32[3,8,128]{2,1,0:T(8,128)S(1)}, f32[3,8,128]{2,1,0:T(8,128)S(1)}, f32[3,16,128]{2,1,0:T(8,128)S(1)}, f32[3,16,128]{2,1,0:T(8,128)S(1)}) custom-call(s32[240]{0:T(256)S(1)} %copy-done, s32[1]{0:T(128)} %get-tuple-element.57.total_ref, f32[17,16,128]{2,1,0:T(8,128)S(1)} %maximum_select_fusion.refs_0_, ...), custom_call_target="tpu_custom_call" | custom-call | tf_op jit(solution)/shard_map/sweep_F/pallas_call | solution.py:296
  81.2 4.8 %collective-permute-done.11 = f32[3,8,128]{2,1,0:T(8,128)S(1)} collective-permute-done((f32[3,8,128]{2,1,0:T(8,128)S(1)}, f32[3,8,128]{2,1,0:T(8,128)S(1)}, u32[]{:S(2)}, u32[]{:S(2)}) %collective-permute-start.11) | collective-permute-done | bytes 12320 | tf_op jit(solution)/shard_map/ppermute | solution.py:76
  92.1 9.7 %sweep_F.7 = (f32[3,8,128]{2,1,0:T(8,128)S(1)}, f32[3,8,128]{2,1,0:T(8,128)S(1)}, f32[3,16,128]{2,1,0:T(8,128)S(1)}, f32[3,16,128]{2,1,0:T(8,128)S(1)}) custom-call(s32[240]{0:T(256)S(1)} %copy-done, s32[1]{0:T(128)} %get-tuple-element.57.total_ref, f32[17,16,128]{2,1,0:T(8,128)S(1)} %maximum_select_fusion.refs_0_, ...), custom_call_target="tpu_custom_call" | custom-call | tf_op jit(solution)/shard_map/sweep_F/pallas_call | solution.py:296
  103.8 4.8 %collective-permute-done.15 = f32[3,8,128]{2,1,0:T(8,128)S(1)} collective-permute-done((f32[3,8,128]{2,1,0:T(8,128)S(1)}, f32[3,8,128]{2,1,0:T(8,128)S(1)}, u32[]{:S(2)}, u32[]{:S(2)}) %collective-permute-start.15) | collective-permute-done | bytes 12320 | tf_op jit(solution)/shard_map/ppermute | solution.py:76
  114.7 9.2 %sweep_F.8 = (f32[3,8,128]{2,1,0:T(8,128)S(1)}, f32[3,8,128]{2,1,0:T(8,128)S(1)}, f32[3,16,128]{2,1,0:T(8,128)S(1)}, f32[3,16,128]{2,1,0:T(8,128)S(1)}) custom-call(s32[240]{0:T(256)S(1)} %copy-done, s32[1]{0:T(128)} %get-tuple-element.57.total_ref, f32[17,16,128]{2,1,0:T(8,128)S(1)} %maximum_select_fusion.refs_0_, ...), custom_call_target="tpu_custom_call" | custom-call | tf_op jit(solution)/shard_map/sweep_F/pallas_call | solution.py:296
  126.0 4.8 %collective-permute-done.19 = f32[3,8,128]{2,1,0:T(8,128)S(1)} collective-permute-done((f32[3,8,128]{2,1,0:T(8,128)S(1)}, f32[3,8,128]{2,1,0:T(8,128)S(1)}, u32[]{:S(2)}, u32[]{:S(2)}) %collective-permute-start.19) | collective-permute-done | bytes 12320 | tf_op jit(solution)/shard_map/ppermute | solution.py:76
  136.9 9.2 %sweep_F.9 = (f32[3,8,128]{2,1,0:T(8,128)S(1)}, f32[3,8,128]{2,1,0:T(8,128)S(1)}, f32[3,16,128]{2,1,0:T(8,128)S(1)}, f32[3,16,128]{2,1,0:T(8,128)S(1)}) custom-call(s32[240]{0:T(256)S(1)} %copy-done, s32[1]{0:T(128)} %get-tuple-element.57.total_ref, f32[17,16,128]{2,1,0:T(8,128)S(1)} %maximum_select_fusion.refs_0_, ...), custom_call_target="tpu_custom_call" | custom-call | tf_op jit(solution)/shard_map/sweep_F/pallas_call | solution.py:296
  159.1 15.7 %sweep_FJ.1 = (f32[6,8,128]{2,1,0:T(8,128)S(1)}, f32[6,8,128]{2,1,0:T(8,128)S(1)}, f32[3,16,128]{2,1,0:T(8,128)S(1)}, f32[3,16,128]{2,1,0:T(8,128)S(1)}, f32[16,128]{1,0:T(8,128)S(1)}) custom-call(s32[240]{0:T(256)S(1)} %copy-done, s32[1]{0:T(128)} %get-tuple-element.57.total_ref, f32[17,16,128]{2,1,0:T(8,128)S(1)} %maximum_select_fusion.refs_0_, ...), custom_call_target="tpu_custom_call" | custom-call | tf_op jit(solution)/shard_map/sweep_FJ/pallas_call | solution.py:296
  176.8 5.0 %collective-permute-done.27 = f32[6,8,128]{2,1,0:T(8,128)S(1)} collective-permute-done((f32[6,8,128]{2,1,0:T(8,128)S(1)}, f32[6,8,128]{2,1,0:T(8,128)S(1)}, u32[]{:S(2)}, u32[]{:S(2)}) %collective-permute-start.27) | collective-permute-done | bytes 24608 | tf_op jit(solution)/shard_map/ppermute | solution.py:76
  188.2 13.6 %sweep_J.5 = (f32[3,8,128]{2,1,0:T(8,128)S(1)}, f32[3,8,128]{2,1,0:T(8,128)S(1)}, f32[3,16,128]{2,1,0:T(8,128)S(1)}, f32[3,16,128]{2,1,0:T(8,128)S(1)}, f32[16,1...) custom-call(s32[240]{0:T(256)S(1)} %copy-done, s32[1]{0:T(128)} %get-tuple-element.57.total_ref, ...), custom_call_target="tpu_custom_call" | custom-call | tf_op jit(solution)/shard_map/sweep_J/pallas_call | solution.py:296
  214.9 13.6 %sweep_J.6 = (f32[3,8,128]{2,1,0:T(8,128)S(1)}, f32[3,8,128]{2,1,0:T(8,128)S(1)}, f32[3,16,128]{2,1,0:T(8,128)S(1)}, f32[3,16,128]{2,1,0:T(8,128)S(1)}, f32[16,128]{1,0:T(8,128)S(1)}) custom-call(s32[240]{0:T(256)S(1)} %copy-done, s32[1]{0:T(128)} %get-tuple-element.57.total_ref, f32[17,16,128]{2,1,0:T(8,128)S(1)} %maximum_select_fusion.refs_0_, ...), custom_call_target="tpu_custom_call" | custom-call | tf_op jit(solution)/shard_map/sweep_J/pallas_call | solution.py:296
  241.6 13.6 %sweep_J.7 = (f32[3,8,128]{2,1,0:T(8,128)S(1)}, f32[3,8,128]{2,1,0:T(8,128)S(1)}, f32[3,16,128]{2,1,0:T(8,128)S(1)}, f32[3,16,128]{2,1,0:T(8,128)S(1)}, f32[16,128]{1,0:T(8,128)S(1)}) custom-call(s32[240]{0:T(256)S(1)} %copy-done, s32[1]{0:T(128)} %get-tuple-element.57.total_ref, f32[17,16,128]{2,1,0:T(8,128)S(1)} %maximum_select_fusion.refs_0_, ...), custom_call_target="tpu_custom_call" | custom-call | tf_op jit(solution)/shard_map/sweep_J/pallas_call | solution.py:296
  268.3 13.6 %sweep_J.8 = (f32[3,8,128]{2,1,0:T(8,128)S(1)}, f32[3,8,128]{2,1,0:T(8,128)S(1)}, f32[3,16,128]{2,1,0:T(8,128)S(1)}, f32[3,16,128]{2,1,0:T(8,128)S(1)}, f32[16,128]{1,0:T(8,128)S(1)}) custom-call(s32[240]{0:T(256)S(1)} %copy-done, s32[1]{0:T(128)} %get-tuple-element.57.total_ref, f32[17,16,128]{2,1,0:T(8,128)S(1)} %maximum_select_fusion.refs_0_, ...), custom_call_target="tpu_custom_call" | custom-call | tf_op jit(solution)/shard_map/sweep_J/pallas_call | solution.py:296
  283.9 4.8 %collective-permute-done.43 = f32[3,8,128]{2,1,0:T(8,128)S(1)} collective-permute-done((f32[3,8,128]{2,1,0:T(8,128)S(1)}, f32[3,8,128]{2,1,0:T(8,128)S(1)}, u32[]{:S(2)}, u32[]{:S(2)}) %collective-permute-start.43) | collective-permute-done | bytes 12320 | tf_op jit(solution)/shard_map/ppermute | solution.py:76
  295.0 13.6 %sweep_J.9 = (f32[3,8,128]{2,1,0:T(8,128)S(1)}, f32[3,8,128]{2,1,0:T(8,128)S(1)}, f32[3,16,128]{2,1,0:T(8,128)S(1)}, f32[3,16,128]{2,1,0:T(8,128)S(1)}, f32[16,128]{1,0:T(8,128)S(1)}) custom-call(s32[240]{0:T(256)S(1)} %copy-done, s32[1]{0:T(128)} %get-tuple-element.57.total_ref, f32[17,16,128]{2,1,0:T(8,128)S(1)} %maximum_select_fusion.refs_0_, ...), custom_call_target="tpu_custom_call" | custom-call | tf_op jit(solution)/shard_map/sweep_J/pallas_call | solution.py:296
  310.7 4.9 %collective-permute-done.47 = f32[4,8,128]{2,1,0:T(8,128)S(1)} collective-permute-done((f32[4,8,128]{2,1,0:T(8,128)S(1)}, f32[4,8,128]{2,1,0:T(8,128)S(1)}, u32[]{:S(2)}, u32[]{:S(2)}) %collective-permute-start.47) | collective-permute-done | bytes 16416 | tf_op jit(solution)/shard_map/ppermute | solution.py:76
  324.0 5.0 %collective-permute-start.51 = (f32[13,128]{1,0:T(8,128)S(1)}, f32[13,128]{1,0:T(8,128)S(1)}, u32[]{:S(2)}, u32[]{:S(2)}) collective-permute-start(f32[13,128]{1,0:T(8,128)S(1)} %bitcast.94), channel_id=1, source_target_pairs={{1,0},{17,1},{49,2},{33,3},{5,4},{21,5},{53,6},{37,7},{9,8},{25,9}... | collective-permute-start | bytes 19976 | tf_op jit(solution)/shard_map/ppermute | solution.py:76
  329.0 8.7 %collective-permute-start.52 = (f32[13,128]{1,0:T(8,128)S(1)}, f32[13,128]{1,0:T(8,128)S(1)}, u32[]{:S(2)}, u32[]{:S(2)}) collective-permute-start(f32[13,128]{1,0:T(8,128)S(1)} %bitcast.93), channel_id=1, source_target_pairs={{2,0},{18,1},{50,2},{34,3},{6,4},{22,5},{54,6},{38,7},{10,8},{26,9... | collective-permute-start | bytes 19976 | tf_op jit(solution)/shard_map/ppermute | solution.py:76
  339.4 6.5 %collective-permute-done.53 = f32[13,128]{1,0:T(8,128)S(1)} collective-permute-done((f32[13,128]{1,0:T(8,128)S(1)}, f32[13,128]{1,0:T(8,128)S(1)}, u32[]{:S(2)}, u32[]{:S(2)}) %collective-permute-start.53) | collective-permute-done | bytes 6688 | tf_op jit(solution)/shard_map/ppermute | solution.py:76
  (246 shorter events, 143.7 us)
Async XLA Ops:
  5.8 16.2 %collective-permute-start.2 = (f32[18,128]{1,0:T(8,128)S(1)}, f32[18,128]{1,0:T(8,128)S(1)}, u32[]{:S(2)}, u32[]{:S(2)}) collective-permute-start(f32[18,128]{1,0:T(8,128)S(1)} %get-tuple-element.129), channel_id=1, source_target_pairs={{0,1},{1,17},{2,49},{3,33},{4,5},{5,21},{6,53},{7,37},{8,9},{9,25}... | collective-permute-start | bytes 27656 | tf_op jit(solution)/shard_map/ppermute | solution.py:76
  11.4 10.6 %collective-permute-start.1 = (f32[18,128]{1,0:T(8,128)S(1)}, f32[18,128]{1,0:T(8,128)S(1)}, u32[]{:S(2)}, u32[]{:S(2)}) collective-permute-start(f32[18,128]{1,0:T(8,128)S(1)} %get-tuple-element.130), channel_id=1, source_target_pairs={{0,2},{1,18},{2,50},{3,34},{4,6},{5,22},{6,54},{7,38},{8,10},{9,26... | collective-permute-start | bytes 27656 | tf_op jit(solution)/shard_map/ppermute | solution.py:76
  16.6 6.8 %collective-permute-start = (f32[18,128]{1,0:T(8,128)S(1)}, f32[18,128]{1,0:T(8,128)S(1)}, u32[]{:S(2)}, u32[]{:S(2)}) collective-permute-start(f32[18,128]{1,0:T(8,128)S(1)} %get-tuple-element.131), channel_id=1, source_target_pairs={{0,3},{1,19},{2,51},{3,35},{4,7},{5,23},{6,55},{7,39},{8,11},{9,27... | collective-permute-start | bytes 27656 | tf_op jit(solution)/shard_map/ppermute | solution.py:76
  19.9 7.7 %collective-permute-start.3 = (f32[18,128]{1,0:T(8,128)S(1)}, f32[18,128]{1,0:T(8,128)S(1)}, u32[]{:S(2)}, u32[]{:S(2)}) collective-permute-start(f32[18,128]{1,0:T(8,128)S(1)} %get-tuple-element.128), channel_id=1, source_target_pairs={{0,0},{1,16},{2,48},{3,32},{4,4},{5,20},{6,52},{7,36},{8,8},{9,24}... | collective-permute-start | bytes 27656 | tf_op jit(solution)/shard_map/ppermute | solution.py:76
  27.8 7.0 %collective-permute-start.4 = (f32[17,4,128]{2,1,0:T(4,128)S(1)}, f32[17,4,128]{2,1,0:T(4,128)S(1)}, u32[]{:S(2)}, u32[]{:S(2)}) collective-permute-start(f32[17,4,128]{2,1,0:T(4,128)S(1)} %slice.278), channel_id=1, source_target_pairs={{16,0},{48,16},{32,48},{4,32},{20,4},{52,20},{36,52},{8,36},{24,8}... | collective-permute-start | bytes 104456 | tf_op jit(solution)/shard_map/ppermute | solution.py:76
  59.3 6.8 %collective-permute-start.7 = (f32[3,8,128]{2,1,0:T(8,128)S(1)}, f32[3,8,128]{2,1,0:T(8,128)S(1)}, u32[]{:S(2)}, u32[]{:S(2)}) collective-permute-start(f32[3,8,128]{2,1,0:T(8,128)S(1)} %get-tuple-element.59), channel_id=1, source_target_pairs={{16,48},{48,16},{32,4},{4,32},{20,52},{52,20},{36,8},{8,36},{24,56... | collective-permute-start | bytes 36872 | tf_op jit(solution)/shard_map/ppermute | solution.py:76
  79.2 6.8 %collective-permute-start.11 = (f32[3,8,128]{2,1,0:T(8,128)S(1)}, f32[3,8,128]{2,1,0:T(8,128)S(1)}, u32[]{:S(2)}, u32[]{:S(2)}) collective-permute-start(f32[3,8,128]{2,1,0:T(8,128)S(1)} %get-tuple-element.63), channel_id=1, source_target_pairs={{16,48},{48,16},{32,4},{4,32},{20,52},{52,20},{36,8},{8,36},{24,56... | collective-permute-start | bytes 36872 | tf_op jit(solution)/shard_map/ppermute | solution.py:76
  101.9 6.8 %collective-permute-start.15 = (f32[3,8,128]{2,1,0:T(8,128)S(1)}, f32[3,8,128]{2,1,0:T(8,128)S(1)}, u32[]{:S(2)}, u32[]{:S(2)}) collective-permute-start(f32[3,8,128]{2,1,0:T(8,128)S(1)} %get-tuple-element.67), channel_id=1, source_target_pairs={{16,48},{48,16},{32,4},{4,32},{20,52},{52,20},{36,8},{8,36},{24,56... | collective-permute-start | bytes 36872 | tf_op jit(solution)/shard_map/ppermute | solution.py:76
  124.1 6.8 %collective-permute-start.19 = (f32[3,8,128]{2,1,0:T(8,128)S(1)}, f32[3,8,128]{2,1,0:T(8,128)S(1)}, u32[]{:S(2)}, u32[]{:S(2)}) collective-permute-start(f32[3,8,128]{2,1,0:T(8,128)S(1)} %get-tuple-element.71), channel_id=1, source_target_pairs={{16,48},{48,16},{32,4},{4,32},{20,52},{52,20},{36,8},{8,36},{24,56... | collective-permute-start | bytes 36872 | tf_op jit(solution)/shard_map/ppermute | solution.py:76
  146.2 6.8 %collective-permute-start.23 = (f32[3,8,128]{2,1,0:T(8,128)S(1)}, f32[3,8,128]{2,1,0:T(8,128)S(1)}, u32[]{:S(2)}, u32[]{:S(2)}) collective-permute-start(f32[3,8,128]{2,1,0:T(8,128)S(1)} %get-tuple-element.75), channel_id=1, source_target_pairs={{16,48},{48,16},{32,4},{4,32},{20,52},{52,20},{36,8},{8,36},{24,56... | collective-permute-start | bytes 36872 | tf_op jit(solution)/shard_map/ppermute | solution.py:76
  174.8 6.9 %collective-permute-start.27 = (f32[6,8,128]{2,1,0:T(8,128)S(1)}, f32[6,8,128]{2,1,0:T(8,128)S(1)}, u32[]{:S(2)}, u32[]{:S(2)}) collective-permute-start(f32[6,8,128]{2,1,0:T(8,128)S(1)} %get-tuple-element.78), channel_id=1, source_target_pairs={{16,48},{48,16},{32,4},{4,32},{20,52},{52,20},{36,8},{8,36},{24,56... | collective-permute-start | bytes 73736 | tf_op jit(solution)/shard_map/ppermute | solution.py:76
  181.8 6.4 %collective-permute-start.28 = (f32[6,8,128]{2,1,0:T(8,128)S(1)}, f32[6,8,128]{2,1,0:T(8,128)S(1)}, u32[]{:S(2)}, u32[]{:S(2)}) collective-permute-start(f32[6,8,128]{2,1,0:T(8,128)S(1)} %pad_maximum_fusion.refs_4_), channel_id=1, source_target_pairs={{0,1},{16,17},{48,49},{32,33},{4,5},{20,21},{52,53},{36,37},{8,9},... | collective-permute-start | bytes 73736 | tf_op jit(solution)/shard_map/ppermute | solution.py:76
  201.9 6.8 %collective-permute-start.31 = (f32[3,8,128]{2,1,0:T(8,128)S(1)}, f32[3,8,128]{2,1,0:T(8,128)S(1)}, u32[]{:S(2)}, u32[]{:S(2)}) collective-permute-start(f32[3,8,128]{2,1,0:T(8,128)S(1)} %get-tuple-element.85), channel_id=1, source_target_pairs={{16,48},{48,16},{32,4},{4,32},{20,52},{52,20},{36,8},{8,36},{24,56... | collective-permute-start | bytes 36872 | tf_op jit(solution)/shard_map/ppermute | solution.py:76
  208.7 6.2 %collective-permute-start.32 = (f32[3,8,128]{2,1,0:T(8,128)S(1)}, f32[3,8,128]{2,1,0:T(8,128)S(1)}, u32[]{:S(2)}, u32[]{:S(2)}) collective-permute-start(f32[3,8,128]{2,1,0:T(8,128)S(1)} %pad_maximum_fusion.16.refs_4_), channel_id=1, source_target_pairs={{0,1},{16,17},{48,49},{32,33},{4,5},{20,21},{52,53},{36,37},{8,9},... | collective-permute-start | bytes 36872 | tf_op jit(solution)/shard_map/ppermute | solution.py:76
  228.6 6.8 %collective-permute-start.35 = (f32[3,8,128]{2,1,0:T(8,128)S(1)}, f32[3,8,128]{2,1,0:T(8,128)S(1)}, u32[]{:S(2)}, u32[]{:S(2)}) collective-permute-start(f32[3,8,128]{2,1,0:T(8,128)S(1)} %get-tuple-element.90), channel_id=1, source_target_pairs={{16,48},{48,16},{32,4},{4,32},{20,52},{52,20},{36,8},{8,36},{24,56... | collective-permute-start | bytes 36872 | tf_op jit(solution)/shard_map/ppermute | solution.py:76
  235.4 6.2 %collective-permute-start.36 = (f32[3,8,128]{2,1,0:T(8,128)S(1)}, f32[3,8,128]{2,1,0:T(8,128)S(1)}, u32[]{:S(2)}, u32[]{:S(2)}) collective-permute-start(f32[3,8,128]{2,1,0:T(8,128)S(1)} %pad_maximum_fusion.18.refs_4_), channel_id=1, source_target_pairs={{0,1},{16,17},{48,49},{32,33},{4,5},{20,21},{52,53},{36,37},{8,9},... | collective-permute-start | bytes 36872 | tf_op jit(solution)/shard_map/ppermute | solution.py:76
  255.3 6.8 %collective-permute-start.39 = (f32[3,8,128]{2,1,0:T(8,128)S(1)}, f32[3,8,128]{2,1,0:T(8,128)S(1)}, u32[]{:S(2)}, u32[]{:S(2)}) collective-permute-start(f32[3,8,128]{2,1,0:T(8,128)S(1)} %get-tuple-element.95), channel_id=1, source_target_pairs={{16,48},{48,16},{32,4},{4,32},{20,52},{52,20},{36,8},{8,36},{24,56... | collective-permute-start | bytes 36872 | tf_op jit(solution)/shard_map/ppermute | solution.py:76
  282.0 6.8 %collective-permute-start.43 = (f32[3,8,128]{2,1,0:T(8,128)S(1)}, f32[3,8,128]{2,1,0:T(8,128)S(1)}, u32[]{:S(2)}, u32[]{:S(2)}) collective-permute-start(f32[3,8,128]{2,1,0:T(8,128)S(1)} %get-tuple-element.100), channel_id=1, source_target_pairs={{16,48},{48,16},{32,4},{4,32},{20,52},{52,20},{36,8},{8,36},{24,56... | collective-permute-start | bytes 36872 | tf_op jit(solution)/shard_map/ppermute | solution.py:76
  308.7 6.8 %collective-permute-start.47 = (f32[4,8,128]{2,1,0:T(8,128)S(1)}, f32[4,8,128]{2,1,0:T(8,128)S(1)}, u32[]{:S(2)}, u32[]{:S(2)}) collective-permute-start(f32[4,8,128]{2,1,0:T(8,128)S(1)} %pad_maximum_fusion.3), channel_id=1, source_target_pairs={{16,48},{48,16},{32,4},{4,32},{20,52},{52,20},{36,8},{8,36},{24,56... | collective-permute-start | bytes 49160 | tf_op jit(solution)/shard_map/ppermute | solution.py:76
  315.6 6.3 %collective-permute-start.48 = (f32[4,8,128]{2,1,0:T(8,128)S(1)}, f32[4,8,128]{2,1,0:T(8,128)S(1)}, u32[]{:S(2)}, u32[]{:S(2)}) collective-permute-start(f32[4,8,128]{2,1,0:T(8,128)S(1)} %pad_maximum_fusion.4), channel_id=1, source_target_pairs={{0,1},{16,17},{48,49},{32,33},{4,5},{20,21},{52,53},{36,37},{8,9},... | collective-permute-start | bytes 49160 | tf_op jit(solution)/shard_map/ppermute | solution.py:76
  322.0 15.8 %collective-permute-start.50 = (f32[13,128]{1,0:T(8,128)S(1)}, f32[13,128]{1,0:T(8,128)S(1)}, u32[]{:S(2)}, u32[]{:S(2)}) collective-permute-start(f32[13,128]{1,0:T(8,128)S(1)} %bitcast.91), channel_id=1, source_target_pairs={{0,0},{16,1},{48,2},{32,3},{4,4},{20,5},{52,6},{36,7},{8,8},{24,9}... | collective-permute-start | bytes 19976 | tf_op jit(solution)/shard_map/ppermute | solution.py:76
  324.0 13.8 %collective-permute-start.51 = (f32[13,128]{1,0:T(8,128)S(1)}, f32[13,128]{1,0:T(8,128)S(1)}, u32[]{:S(2)}, u32[]{:S(2)}) collective-permute-start(f32[13,128]{1,0:T(8,128)S(1)} %bitcast.94), channel_id=1, source_target_pairs={{1,0},{17,1},{49,2},{33,3},{5,4},{21,5},{53,6},{37,7},{9,8},{25,9}... | collective-permute-start | bytes 19976 | tf_op jit(solution)/shard_map/ppermute | solution.py:76
  329.0 10.4 %collective-permute-start.52 = (f32[13,128]{1,0:T(8,128)S(1)}, f32[13,128]{1,0:T(8,128)S(1)}, u32[]{:S(2)}, u32[]{:S(2)}) collective-permute-start(f32[13,128]{1,0:T(8,128)S(1)} %bitcast.93), channel_id=1, source_target_pairs={{2,0},{18,1},{50,2},{34,3},{6,4},{22,5},{54,6},{38,7},{10,8},{26,9... | collective-permute-start | bytes 19976 | tf_op jit(solution)/shard_map/ppermute | solution.py:76
  337.7 8.2 %collective-permute-start.53 = (f32[13,128]{1,0:T(8,128)S(1)}, f32[13,128]{1,0:T(8,128)S(1)}, u32[]{:S(2)}, u32[]{:S(2)}) collective-permute-start(f32[13,128]{1,0:T(8,128)S(1)} %bitcast.92), channel_id=1, source_target_pairs={{3,0},{19,1},{51,2},{35,3},{7,4},{23,5},{55,6},{39,7},{11,8},{27,9... | collective-permute-start | bytes 19976 | tf_op jit(solution)/shard_map/ppermute | solution.py:76
  (42 other events, 96.9 us)
